TPU v7x, 128 devices: a whole 4x4x4 slice. The times are simulated.
128 devices in a mesh: dp: 2 (over x_lo), tm: 16 (over z, y), head: 4 (over x_hi, core).
Axes of the slice: x: 4 (x_hi: 2, x_lo: 2; x = x_hi * 2 + x_lo), y: 4, z: 4, core: 2. Of those that a mesh axis runs over, the one named last changes fastest.
Arguments:
- clip: bfloat16 [32, 1792, 1152], P(('dp', 'tm'), 'head'), parts along dimension 0, may hold values from -8 to 8
- modulation: float32 [12, 1152], P('dp'), parts along dimension 0, may hold values from -3 to 3
- w_qkv_s: bfloat16 [1152, 3456], replicated, may hold values from -1.9 to 1.9
- w_out_s: bfloat16 [1152, 1152], replicated, may hold values from -0.1875 to 0.1875
- w_qkv_t: bfloat16 [1152, 3456], replicated, may hold values from -1.9 to 1.9
- w_out_t: bfloat16 [1152, 1152], replicated, may hold values from -0.1875 to 0.1875
Outputs:
- result: bfloat16 [32, 1792, 1152], P(('dp', 'tm'), 'head'), parts along dimension 0
There are 2 independent parts, one for each index of `dp`. A program takes and returns all parts, laid end to end along the dimension named above; an argument that names none is the same for every part. Nothing has to cross between parts.
All inputs are finite; a program needn't handle non-finite values.
Results may differ from a plain program's by a relative error of at most 0.017.
Values may be sent and summed in bfloat16 or wider, within the bound.
No kernel may reach another device: no remote copies, remote signals or barrier semaphores. Data moves between devices by JAX's collectives and lax.ppermute only.
A program may use at most 192 MiB of HBM per device.

v0:
```python
import math

import jax
import jax.numpy as jnp
from jax import lax
from jax.sharding import PartitionSpec as P

HEADS = 16


def modulate(tokens, shift_vec, scale_vec):
    values = tokens.astype(jnp.float32)
    average = jnp.mean(values, axis=-1, keepdims=True)
    centred = values - average
    variance = jnp.mean(centred * centred, axis=-1, keepdims=True)
    normed = centred / jnp.sqrt(variance + 1e-06)
    return (normed * (1.0 + scale_vec) + shift_vec).astype(jnp.bfloat16)


def attend_core(queries, key_rows, values):
    scores = jnp.einsum(
        "nqe,nke->nqk", queries, key_rows, preferred_element_type=jnp.float32
    ) / math.sqrt(queries.shape[-1])
    row_max = jnp.max(scores, axis=-1, keepdims=True)
    weights = jnp.exp(scores - row_max)
    row_total = jnp.sum(weights, axis=-1, keepdims=True)
    rounded = weights.astype(jnp.bfloat16)
    attended = jnp.einsum("nqk,nke->nqe", rounded, values, preferred_element_type=jnp.float32)
    return (attended / row_total).astype(jnp.bfloat16)


def attend_each(queries, key_rows, values):

    def single(trio):
        return attend_core(trio[0][None], trio[1][None], trio[2][None])[0]

    return lax.map(single, (queries, key_rows, values))


def project_add(tokens, attended, w_out, gate_vec):
    frames, tokens_dev, model_width = tokens.shape
    projected = jnp.dot(
        attended.reshape(frames * tokens_dev, model_width),
        w_out,
        preferred_element_type=jnp.float32,
    )
    projected = projected.reshape(frames, tokens_dev, model_width)
    return (tokens.astype(jnp.float32) + gate_vec * projected).astype(jnp.bfloat16)


def local(clip, modulation, w_qkv_s, w_out_s, w_qkv_t, w_out_t):
    frames, tokens_dev, model_width = clip.shape
    head_dim = model_width // HEADS
    normed = modulate(clip, modulation[0], modulation[1])
    packed = jnp.dot(
        normed.reshape(frames * tokens_dev, model_width),
        w_qkv_s,
        preferred_element_type=jnp.float32,
    )
    packed = packed.astype(jnp.bfloat16).reshape(frames, tokens_dev, 3 * model_width)
    groups = lax.axis_size("head")
    group_cols = model_width // groups
    grouped = packed.reshape(frames, tokens_dev, 3, groups, group_cols)
    block = lax.all_to_all(grouped, "head", split_axis=3, concat_axis=1, tiled=True)
    count = block.shape[0]
    seq_len = block.shape[1]
    local_heads = group_cols // head_dim
    arranged = block.reshape(count, seq_len, 3, local_heads, head_dim).transpose(2, 0, 3, 1, 4)
    arranged = arranged.reshape(3, count * local_heads, seq_len, head_dim)
    attended = attend_each(arranged[0], arranged[1], arranged[2])
    attended = attended.reshape(count, local_heads, seq_len, head_dim).transpose(0, 2, 1, 3)
    attended = attended.reshape(count, seq_len, 1, group_cols)
    returned = lax.all_to_all(attended, "head", split_axis=1, concat_axis=2, tiled=True)
    attended_s = returned.reshape(count, returned.shape[1], model_width)
    middle = project_add(clip, attended_s, w_out_s, modulation[2])
    normed_t = modulate(middle, modulation[3], modulation[4])
    packed_t = jnp.dot(
        normed_t.reshape(frames * tokens_dev, model_width),
        w_qkv_t,
        preferred_element_type=jnp.float32,
    )
    time_groups = lax.axis_size("tm")
    packed_t = packed_t.astype(jnp.bfloat16).reshape(
        frames, time_groups, tokens_dev // time_groups, 3 * model_width
    )
    block = lax.all_to_all(packed_t, "tm", split_axis=1, concat_axis=0, tiled=True)
    all_frames = block.shape[0]
    count = block.shape[2]
    arranged = block.reshape(all_frames, count, 3, HEADS, head_dim).transpose(2, 1, 3, 0, 4)
    arranged = arranged.reshape(3, count * HEADS, all_frames, head_dim)
    attended = attend_core(arranged[0], arranged[1], arranged[2])
    attended = attended.reshape(count, HEADS, all_frames, head_dim).transpose(2, 0, 1, 3)
    attended = attended.reshape(all_frames, 1, count, model_width)
    attended_t = lax.all_to_all(attended, "tm", split_axis=0, concat_axis=1, tiled=True)
    attended_t = attended_t.reshape(frames, tokens_dev, model_width)
    return project_add(middle, attended_t, w_out_t, modulation[5])


def solution(mesh):
    placed = (P(("dp", "tm"), "head", None), P("dp", None), P(), P(), P(), P())
    return jax.shard_map(
        local, mesh=mesh, in_specs=placed, out_specs=P(("dp", "tm"), "head", None), check_vma=False
    )
```

profile of v0, /device:TPU:0, one launch (start us, length us, event | category | flops | bytes accessed | tf_op | source)
XLA Modules:
  0.0 315.2 jit_solution(7280976620025346294)
XLA Ops:
  0.0 0.0 copy-start
  0.0 1.2 slice_reduce_fusion.1
  1.2 1.4 convert_reduce_fusion.1
  2.6 1.6 fusion.42
  4.3 9.9 %convolution_convert_fusion.1 = bf16[448,3456]{1,0:T(8,128)(2,1)} fusion(bf16[1152,3456]{1,0:T(8,128)(2,1)} %param.10, bf16[1,448,1152]{2,1,0:T(8,128)(2,1)} %param.8, f32[1152]{0:T(1024)S(1)} %get-tuple-element.54, f32[1152]{0:T(1024)S(1)} %get-tuple-element.55, f32[448]{0:T(512)S(1)} %add_sqrt_fusion.1, f32[448]{0:T(512)S(1)} %broadcast_multiply_fusion.1), kind=kOutput, calls=%fused_computation.20 | convolution fusion | flops 3571900416 | bytes 12104192 | tf_op jit(solution)/shard_map/dot_general | solution.py:55
  14.1 5.6 %copy.51 = bf16[448,3456]{0,1:T(8,128)(2,1)} copy(bf16[448,3456]{1,0:T(8,128)(2,1)} %convolution_convert_fusion.1) | data formatting | bytes 6193152 | tf_op jit(solution)/shard_map/convert_element_type | solution.py:60
  19.7 4.0 %copy.52 = bf16[1,448,3,4,288]{1,4,2,0,3:T(8,128)(2,1)} copy(bf16[1,448,3,4,288]{1,4,3,2,0:T(8,128)(2,1)} %bitcast.99) | data formatting | bytes 6193152 | tf_op jit(solution)/shard_map/reshape;reshape | solution.py:63
  23.8 4.9 %all-to-all-start = ((bf16[1,448,3,4,288]{1,4,2,0,3:T(8,128)(2,1)}), bf16[1,448,3,4,288]{1,4,2,0,3:T(8,128)(2,1)}, u32[]{:S(2)}, u32[]{:S(2)}) async-start(bf16[1,448,3,4,288]{1,4,2,0,3:T(8,128)(2,1)} %copy.52), calls=%async_computation | async-start | bytes 7077888 | tf_op jit(solution)/shard_map/all_to_all | solution.py:64
  28.7 42.5 %all-to-all-done = bf16[1,448,3,4,288]{1,4,2,0,3:T(8,128)(2,1)} async-done(((bf16[1,448,3,4,288]{1,4,2,0,3:T(8,128)(2,1)}), bf16[1,448,3,4,288]{1,4,2,0,3:T(8,128)(2,1)}, u32[]{:S(2)}, u32[]{:S(2)}) %all-to-all-start) | async-done | bytes 3096608 | tf_op jit(solution)/shard_map/all_to_all | solution.py:64
  71.2 6.5 %copy.53 = bf16[1,4,448,3,1,288]{2,1,5,3,4,0:T(4,128)(2,1)} copy(bf16[1,4,448,3,1,288]{2,5,3,1,4,0:T(8,128)(2,1)} %bitcast.7) | data formatting | bytes 6193152 | tf_op jit(solution)/shard_map/all_to_all | solution.py:64
  77.7 6.8 %reshape.161 = bf16[1,1792,3,4,72]{1,4,3,2,0:T(8,128)(2,1)} reshape(bf16[1,4,448,3,1,288]{2,1,5,3,4,0:T(4,128)(2,1)} %copy.53) | data formatting | bytes 6193152 | tf_op jit(solution)/shard_map/reshape | solution.py:68
  84.5 3.6 %slice_bitcast_fusion = (bf16[4,1792,72]{1,2,0:T(8,128)(2,1)}, bf16[4,1792,72]{1,2,0:T(8,128)(2,1)}, bf16[4,1792,72]{1,2,0:T(8,128)(2,1)}) fusion(bf16[3,1,4,1792,72]{3,4,2,0,1:T(8,128)(2,1)} %bitcast.101), kind=kLoop, calls=%fused_computation.55 | loop fusion | bytes 6193152 | tf_op jit(solution)/shard_map/squeeze | solution.py:70
  88.1 35.9 %while.10 = (s32[]{:T(128)}, bf16[4,1792,72]{1,2,0:T(8,128)(2,1)}, bf16[4,1792,72]{1,2,0:T(8,128)(2,1)}, bf16[4,1792,72]{1,2,0:T(8,128)(2,1)}, bf16[4,1792,72]{1,2,0:T(8,128)(2,1)}, /*index=5*/s32[]{:T(128)}) while((s32[]{:T(128)}, bf16[4,1792,72]{1,2,0:T(8,128)(2,1)}, bf16[4,1792,72]{1,2,0:T(8,128)(2,1)}, bf16[4,1792,72]{1,2,0:T(8,128)(2,1)}, ...), condition=%wide.region_5.6_spmd, body=%wide.region_2.5_spmd.sunk | while | flops 950788608 | bytes 39605316 | solution.py:37
  88.1 3.0 multiply_reduce_fusion.3
  91.1 2.1 fusion.78
  93.2 3.9 %fusion.79 = bf16[4,1792,72]{1,2,0:T(8,128)(2,1)} fusion(bf16[4,1792,72]{1,2,0:T(8,128)(2,1)} %get-tuple-element.123, s32[]{:T(128)} %get-tuple-element.122, f32[1792,1792]{0,1:T(8,128)S(1)} %get-tuple-element.114, f32[1792]{0:T(1024)S(1)} %get-tuple-element.115, f32[1792]{0:T(1024)S(1)} %fusion.78, bf16[4,1792,72]{1,2,0:T(8,128)(2,1)} %get-tuple-element.132), kind=kOutput, calls=%fused_computation.8.clone.1 | convolution fusion | flops 472313856 | bytes 13376512 | tf_op jit(solution)/shard_map/while/body/eval_jaxpr/nqk,nke->nqe/dot_general | solution.py:28
  97.1 3.0 multiply_reduce_fusion.3
  100.1 2.1 fusion.78
  102.2 3.9 %fusion.79 = bf16[4,1792,72]{1,2,0:T(8,128)(2,1)} fusion(bf16[4,1792,72]{1,2,0:T(8,128)(2,1)} %get-tuple-element.123, s32[]{:T(128)} %get-tuple-element.122, f32[1792,1792]{0,1:T(8,128)S(1)} %get-tuple-element.114, f32[1792]{0:T(1024)S(1)} %get-tuple-element.115, f32[1792]{0:T(1024)S(1)} %fusion.78, bf16[4,1792,72]{1,2,0:T(8,128)(2,1)} %get-tuple-element.132), kind=kOutput, calls=%fused_computation.8.clone.1 | convolution fusion | flops 472313856 | bytes 13376512 | tf_op jit(solution)/shard_map/while/body/eval_jaxpr/nqk,nke->nqe/dot_general | solution.py:28
  106.1 3.0 multiply_reduce_fusion.3
  109.1 2.1 fusion.78
  111.2 3.9 %fusion.79 = bf16[4,1792,72]{1,2,0:T(8,128)(2,1)} fusion(bf16[4,1792,72]{1,2,0:T(8,128)(2,1)} %get-tuple-element.123, s32[]{:T(128)} %get-tuple-element.122, f32[1792,1792]{0,1:T(8,128)S(1)} %get-tuple-element.114, f32[1792]{0:T(1024)S(1)} %get-tuple-element.115, f32[1792]{0:T(1024)S(1)} %fusion.78, bf16[4,1792,72]{1,2,0:T(8,128)(2,1)} %get-tuple-element.132), kind=kOutput, calls=%fused_computation.8.clone.1 | convolution fusion | flops 472313856 | bytes 13376512 | tf_op jit(solution)/shard_map/while/body/eval_jaxpr/nqk,nke->nqe/dot_general | solution.py:28
  115.1 3.0 multiply_reduce_fusion.3
  118.0 2.1 fusion.78
  120.2 3.9 %fusion.79 = bf16[4,1792,72]{1,2,0:T(8,128)(2,1)} fusion(bf16[4,1792,72]{1,2,0:T(8,128)(2,1)} %get-tuple-element.123, s32[]{:T(128)} %get-tuple-element.122, f32[1792,1792]{0,1:T(8,128)S(1)} %get-tuple-element.114, f32[1792]{0:T(1024)S(1)} %get-tuple-element.115, f32[1792]{0:T(1024)S(1)} %fusion.78, bf16[4,1792,72]{1,2,0:T(8,128)(2,1)} %get-tuple-element.132), kind=kOutput, calls=%fused_computation.8.clone.1 | convolution fusion | flops 472313856 | bytes 13376512 | tf_op jit(solution)/shard_map/while/body/eval_jaxpr/nqk,nke->nqe/dot_general | solution.py:28
  124.1 6.6 %copy.57 = bf16[1,1792,1,288]{3,2,0,1:T(2,128)(2,1)} copy(bf16[1,1792,1,288]{1,3,2,0:T(8,128)(2,1)} %bitcast.14) | data formatting | bytes 2064384 | tf_op jit(solution)/shard_map/reshape | solution.py:72
  130.7 0.5 broadcast.109
  131.2 13.6 %reduce.20 = bf16[1792,288]{1,0:T(8,128)(2,1)} reduce(bf16[1792,1,1,288]{3,2,1,0:T(2,128)(2,1)} %bitcast.102, bf16[]{:T(256)} %broadcast.109), dimensions={1,2}, to_apply=%bitcast.74.reduce_sub_computation | reduce | bytes 2064386
  144.9 4.4 %reshape.175 = bf16[4,2,64512]{2,1,0:T(2,128)(2,1)} reshape(bf16[1792,288]{1,0:T(8,128)(2,1)} %reduce.20) | data formatting | bytes 2064384
  149.3 20.1 %all_to_all.48 = bf16[4,2,64512]{2,1,0:T(2,128)(2,1)} all-to-all(bf16[4,2,64512]{2,1,0:T(2,128)(2,1)} %reshape.175), channel_id=1, replica_groups=mesh['dp'=2,'tm'=16,'head'=4] {'head'}, dimensions={0} | all-to-all | bytes 2064384 | tf_op jit(solution)/shard_map/all_to_all | solution.py:73
  169.4 4.8 %reshape.176 = bf16[1792,1,1,288]{3,2,1,0:T(2,128)(2,1)} reshape(bf16[4,2,64512]{2,1,0:T(2,128)(2,1)} %all_to_all.48) | data formatting | bytes 2064384
  174.2 6.6 %copy.58 = bf16[1,1792,1,288]{1,3,2,0:T(8,128)(2,1)} copy(bf16[1,1792,1,288]{3,2,0,1:T(2,128)(2,1)} %bitcast.103) | data formatting | bytes 2064384 | tf_op jit(solution)/shard_map/all_to_all | solution.py:73
  180.8 3.2 %all_to_all.40 = bf16[1,4,448,1,288]{2,1,4,3,0:T(4,128)(2,1)} reshape(bf16[1,1792,1,288]{1,3,2,0:T(8,128)(2,1)} %copy.58) | data formatting | bytes 2064384 | tf_op jit(solution)/shard_map/all_to_all | solution.py:73
  184.0 1.5 copy.59
  185.5 0.0 copy-done
  185.5 3.1 convert_reduce_fusion
  188.6 0.0 copy-start.1
  188.6 0.4 fusion.38
  189.0 0.6 copy-done.1
  189.6 9.4 %convolution_convert_fusion = bf16[448,3456]{1,0:T(8,128)(2,1)} fusion(bf16[1152,3456]{1,0:T(8,128)(2,1)} %param.12, bf16[1,448,1152]{2,1,0:T(8,128)(2,1)S(1)} %get-tuple-element.78, f32[1152]{0:T(1024)S(1)} %get-tuple-element.57, f32[1152]{0:T(1024)S(1)} %get-tuple-element.58, f32[448]{0:T(512)S(1)} %add_sqrt_fusion, f32[448]{0:T(512)S(1)} %broadcast_multiply_fusion), kind=kOutput, calls=%fused_computation.19 | convolution fusion | flops 3571900416 | bytes 12104192 | tf_op jit(solution)/shard_map/dot_general | solution.py:77
  199.1 4.5 %reshape.165 = bf16[1,16,28,3456]{3,2,1,0:T(8,128)(2,1)} reshape(bf16[448,3456]{1,0:T(8,128)(2,1)} %convolution_convert_fusion) | data formatting | bytes 6193152 | tf_op jit(solution)/shard_map/reshape | solution.py:83
  203.5 51.7 %all_to_all.49 = bf16[1,16,28,3456]{3,2,0,1:T(8,128)(2,1)S(1)} all-to-all(bf16[1,16,28,3456]{3,2,0,1:T(8,128)(2,1)} %bitcast.100), channel_id=1, replica_groups=mesh['dp'=2,'tm'=16,'head'=4] {'tm'}, dimensions={1} | all-to-all | bytes 6193152 | tf_op jit(solution)/shard_map/all_to_all | solution.py:86
  255.2 2.5 copy.61
  257.8 11.4 %reshape.166 = bf16[16,28,3,16,72]{4,3,2,0,1:T(8,128)(2,1)} reshape(bf16[1,16,28,3456]{3,1,2,0:T(8,128)(2,1)} %copy.61) | data formatting | bytes 6193152 | tf_op jit(solution)/shard_map/reshape | solution.py:89
  269.2 4.0 %fusion.62 = (bf16[1,28,16,16,72]{4,2,0,3,1:T(8,128)(2,1)S(1)}, bf16[1,28,16,16,72]{4,2,0,3,1:T(8,128)(2,1)S(1)}, bf16[1,28,16,16,72]{4,2,0,3,1:T(8,128)(2,1)S(1)}) fusion(bf16[3,28,16,16,72]{4,2,0,3,1:T(8,128)(2,1)} %bitcast.98), kind=kLoop, calls=%fused_computation.77 | loop fusion | bytes 6193152 | tf_op jit(solution)/shard_map/slice | solution.py:91
  273.2 0.5 copy.62
  273.7 0.5 copy.63
  274.2 0.5 copy.64
  274.7 1.1 multiply_reduce_fusion.1
  275.8 1.4 fusion.30
  277.2 2.6 divide_convert_fusion
  279.8 1.7 copy.73
  281.5 4.2 %reshape.168 = bf16[16,1,28,1152]{3,0,2,1:T(8,128)(2,1)} reshape(bf16[16,28,16,72]{3,2,0,1:T(8,128)(2,1)} %bitcast.104) | data formatting | bytes 2064384 | tf_op jit(solution)/shard_map/reshape | solution.py:93
  285.7 1.4 copy.67
  287.1 21.0 %all_to_all.50 = bf16[16,1,28,1152]{3,2,1,0:T(8,128)(2,1)} all-to-all(bf16[16,1,28,1152]{3,2,1,0:T(8,128)(2,1)S(1)} %copy.67), channel_id=1, replica_groups=mesh['dp'=2,'tm'=16,'head'=4] {'tm'}, dimensions={0} | all-to-all | bytes 2064384 | tf_op jit(solution)/shard_map/all_to_all | solution.py:94
  308.1 2.2 reshape_reshape.11
  310.3 4.9 %fusion.32 = bf16[1,448,1152]{2,1,0:T(8,128)(2,1)} fusion(bf16[448,1152]{1,0:T(8,128)(2,1)} %reshape_reshape.11, bf16[1152,1152]{1,0:T(8,128)(2,1)} %param.13, bf16[1,448,1152]{2,1,0:T(8,128)(2,1)} %copy-done.1, f32[1152]{0:T(1024)S(1)} %get-tuple-element.53), kind=kOutput, calls=%fused_computation.36 | convolution fusion | flops 1191149568 | bytes 5755392 | tf_op jit(solution)/shard_map/dot_general | solution.py:42
  (5 shorter events, 0.0 us)
Async XLA Ops:
  0.0 185.5 %copy-start = (bf16[1152,1152]{1,0:T(8,128)(2,1)S(1)}, bf16[1152,1152]{1,0:T(8,128)(2,1)}, u32[]{:S(2)}) copy-start(bf16[1152,1152]{1,0:T(8,128)(2,1)} %param.11) | copy-start | bytes 7962628
  23.8 47.4 %all-to-all-start = ((bf16[1,448,3,4,288]{1,4,2,0,3:T(8,128)(2,1)}), bf16[1,448,3,4,288]{1,4,2,0,3:T(8,128)(2,1)}, u32[]{:S(2)}, u32[]{:S(2)}) async-start(bf16[1,448,3,4,288]{1,4,2,0,3:T(8,128)(2,1)} %copy.52), calls=%async_computation | async-start | bytes 7077888 | tf_op jit(solution)/shard_map/all_to_all | solution.py:64
  188.6 1.1 copy-start.1
where the time goes:
time: 317 us; the launch traced here: 315 us
  blocking collectives  92.7 us (29%)
  local copies, waits for them, and re-layouts  88.2 us (28%)
  matrix products  58.3 us (18%)
  waiting for transfers between devices  42.5 us (13%)
  other arithmetic  28.3 us (9%)
  starting transfers between devices  4.91 us (2%)
    all_to_all x1, blocking collectives, local(): lax.all_to_all(packed_t, 'tm', split_axis=1, concat_axis=0, tiled=True)  51.7 us
    all_to_all x1, waiting for transfers between devices, local(): lax.all_to_all(grouped, 'head', split_axis=3, concat_axis=1, tiled=True)  42.5 us
    all_to_all x1, blocking collectives, local(): lax.all_to_all(attended, 'tm', split_axis=0, concat_axis=1, tiled=True)  21 us
    all_to_all x1, blocking collectives, local(): lax.all_to_all(attended, 'head', split_axis=1, concat_axis=2, tiled=True)  20.1 us
    dot_general x5, matrix products, attend_core(): jnp.einsum('nqk,nke->nqe', rounded, values, preferred_element_type=jnp.fl...  18.1 us
    unnamed x1, other arithmetic  13.6 us
    dot_general x5, matrix products, attend_core(): jnp.einsum('nqe,nke->nqk', queries, key_rows, preferred_element_type=jnp....  12.9 us
    reshape x1, local copies, waits for them, and re-layouts, local(): block.reshape(all_frames, count, 3, HEADS, head_dim)  11.4 us
  transfers between devices with their start and end apart: 1, of which 1 were waited for; matrix products, arithmetic and copies ran while one was open for 0% of the time, Pallas kernels for 0%

commit v1 on v0

v1 whole, which is shorter than its diff:
```python
import functools
import math

import jax
import jax.numpy as jnp
from jax import lax
from jax.experimental import pallas as pl
from jax.experimental.pallas import tpu as pltpu
from jax.sharding import PartitionSpec as P

HEADS = 16
PAIRS = 8
HEAD_DIM = 72
PAIR_COLS = 144
WIDTH = 1152
ROWS = 448
LANES = 896
AUG = 80
QSCALE = math.log2(math.e) / math.sqrt(HEAD_DIM)
NT = (((1,), (1,)), ((), ()))
VMEM_LIMIT = 58 * 1024 * 1024


def modulate(values, shift_vec, scale_vec):
    values = values.astype(jnp.float32)
    average = jnp.mean(values, axis=-1, keepdims=True)
    centred = values - average
    variance = jnp.mean(centred * centred, axis=-1, keepdims=True)
    normed = centred * lax.rsqrt(variance + 1e-06)
    return (normed * (1.0 + scale_vec) + shift_vec).astype(jnp.bfloat16)


def key_phase(x_refs, mod_ref, wk_ref, xn_ref, k_ref):
    for i, x_ref in enumerate(x_refs):
        rows = pl.ds(i * ROWS, ROWS)
        xn_ref[rows, :] = modulate(x_ref[...], mod_ref[0:1, :], mod_ref[1:2, :])
        k_ref[rows, :] = jnp.dot(
            xn_ref[rows, :], wk_ref[...], preferred_element_type=jnp.float32
        ).astype(jnp.bfloat16)


def attend_pair(pair, xn_ref, k_ref, wvt_ref, qq_ref, tile):
    keys = xn_ref.shape[0]
    vt = lax.dot_general(wvt_ref[...], xn_ref[...], NT, preferred_element_type=jnp.float32)
    first = lax.broadcasted_iota(jnp.int32, (AUG - HEAD_DIM, keys), 0) == 0
    tail = jnp.where(first, 1.0, 0.0)
    va = jnp.concatenate([vt[:HEAD_DIM], tail], axis=0).astype(jnp.bfloat16)
    vb = jnp.concatenate([vt[HEAD_DIM:], tail], axis=0).astype(jnp.bfloat16)
    kw = k_ref[:, pl.ds(pl.multiple_of(pair * 128, 128), 256)]
    starts = list(range(0, LANES, tile))

    def score(start):
        width = min(tile, LANES - start)
        return jnp.dot(kw, qq_ref[:, start : start + width], preferred_element_type=jnp.float32)

    out = []
    ahead = score(starts[0])
    for i, start in enumerate(starts):
        scores = ahead
        if i + 1 < len(starts):
            ahead = score(starts[i + 1])
        width = scores.shape[1]
        top = jnp.max(scores, axis=0, keepdims=True)
        weights = jnp.exp2(scores - top).astype(jnp.bfloat16)
        if start + width <= ROWS:
            total = jnp.dot(va, weights, preferred_element_type=jnp.float32)
        elif start >= ROWS:
            total = jnp.dot(vb, weights, preferred_element_type=jnp.float32)
        else:
            lane = lax.broadcasted_iota(jnp.int32, (AUG, width), 1)
            total = jnp.where(
                lane < ROWS - start,
                jnp.dot(va, weights, preferred_element_type=jnp.float32),
                jnp.dot(vb, weights, preferred_element_type=jnp.float32),
            )
        out.append((start, width, total, top))
    return out


def near_kernel(tile, xo_ref, xp_ref, mod_ref, wk_ref, wqt_ref, wvt_ref, qq_ref, acc_ref, top_ref, xn_ref, k_ref):
    pair = pl.program_id(0)

    @pl.when(pair == 0)
    def _():
        key_phase((xo_ref, xp_ref), mod_ref, wk_ref, xn_ref, k_ref)

    qt = lax.dot_general(wqt_ref[...], xn_ref[0:ROWS, :], NT, preferred_element_type=jnp.float32) * QSCALE
    zero = jnp.zeros((HEAD_DIM, ROWS), jnp.float32)
    qa = jnp.concatenate([qt[:HEAD_DIM], zero], axis=0).astype(jnp.bfloat16)
    qb = jnp.concatenate([zero, qt[HEAD_DIM:]], axis=0).astype(jnp.bfloat16)
    qq_ref[...] = jnp.zeros_like(qq_ref)
    place = pl.ds(pl.multiple_of(pair * 16, 16), PAIR_COLS)
    qq_ref[place, :] = jnp.concatenate([qa, qb], axis=1)
    for start, width, total, top in attend_pair(pair, xn_ref, k_ref, wvt_ref, qq_ref, tile):
        acc_ref[:, start : start + width] = total
        top_ref[:, start : start + width] = jnp.broadcast_to(top, (8, width))


def far_kernel(
    tile, xa_ref, xb_ref, xo_ref, mod_ref, wk_ref, wvt_ref, wo_ref, qq_ref, acc_ref, top_ref, out_ref, xn_ref, k_ref, att_ref
):
    pair = pl.program_id(0)

    @pl.when(pair == 0)
    def _():
        key_phase((xa_ref, xb_ref), mod_ref, wk_ref, xn_ref, k_ref)

    parts = []
    for start, width, total, top in attend_pair(pair, xn_ref, k_ref, wvt_ref, qq_ref, tile):
        old_top = top_ref[0:1, start : start + width]
        new_top = jnp.maximum(old_top, top)
        total = total * jnp.exp2(top - new_top) + acc_ref[:, start : start + width] * jnp.exp2(old_top - new_top)
        parts.append(total[:HEAD_DIM] / total[HEAD_DIM : HEAD_DIM + 1])
    merged = jnp.concatenate(parts, axis=1)
    both = jnp.concatenate([merged[:, :ROWS], merged[:, ROWS:]], axis=0).astype(jnp.bfloat16)
    att_ref[pl.ds(pl.multiple_of(pair * PAIR_COLS, 16), PAIR_COLS), :] = both

    @pl.when(pair == PAIRS - 1)
    def _():
        projected = lax.dot_general(
            att_ref[...], wo_ref[...], (((0,), (0,)), ((), ())), preferred_element_type=jnp.float32
        )
        middle = xo_ref[...].astype(jnp.float32) + mod_ref[2:3, :] * projected
        for d in range(16):
            piece = jnp.concatenate([middle[28 * d : 28 * d + 28], jnp.zeros((4, WIDTH), jnp.float32)], axis=0)
            out_ref[d] = piece.astype(jnp.bfloat16)


def whole(shape):
    return pl.BlockSpec(shape, lambda p: (0,) * len(shape))


def near(xo, xp, mod, wk, wqt, wvt, tile=256):
    return pl.pallas_call(
        functools.partial(near_kernel, tile),
        grid=(PAIRS,),
        in_specs=[
            whole((ROWS, WIDTH)),
            whole((ROWS, WIDTH)),
            whole((6, WIDTH)),
            whole((WIDTH, WIDTH)),
            pl.BlockSpec((PAIR_COLS, WIDTH), lambda p: (p, 0)),
            pl.BlockSpec((PAIR_COLS, WIDTH), lambda p: (p, 0)),
        ],
        out_specs=[
            pl.BlockSpec((None, 256, LANES), lambda p: (p, 0, 0)),
            pl.BlockSpec((None, AUG, LANES), lambda p: (p, 0, 0)),
            pl.BlockSpec((None, 8, LANES), lambda p: (p, 0, 0)),
        ],
        out_shape=[
            jax.ShapeDtypeStruct((PAIRS, 256, LANES), jnp.bfloat16),
            jax.ShapeDtypeStruct((PAIRS, AUG, LANES), jnp.float32),
            jax.ShapeDtypeStruct((PAIRS, 8, LANES), jnp.float32),
        ],
        scratch_shapes=[pltpu.VMEM((2 * ROWS, WIDTH), jnp.bfloat16), pltpu.VMEM((2 * ROWS, WIDTH), jnp.bfloat16)],
        compiler_params=pltpu.CompilerParams(vmem_limit_bytes=VMEM_LIMIT),
        cost_estimate=pl.CostEstimate(flops=20_000_000_000, bytes_accessed=20_000_000, transcendentals=6_400_000),
        name="near_tokens",
    )(xo, xp, mod, wk, wqt, wvt)


def far(xa, xb, xo, mod, wk, wvt, wo, qq, acc, top, tile=256):
    return pl.pallas_call(
        functools.partial(far_kernel, tile),
        grid=(PAIRS,),
        in_specs=[
            whole((ROWS, WIDTH)),
            whole((ROWS, WIDTH)),
            whole((ROWS, WIDTH)),
            whole((6, WIDTH)),
            whole((WIDTH, WIDTH)),
            pl.BlockSpec((PAIR_COLS, WIDTH), lambda p: (p, 0)),
            whole((WIDTH, WIDTH)),
            pl.BlockSpec((None, 256, LANES), lambda p: (p, 0, 0)),
            pl.BlockSpec((None, AUG, LANES), lambda p: (p, 0, 0)),
            pl.BlockSpec((None, 8, LANES), lambda p: (p, 0, 0)),
        ],
        out_specs=whole((16, 32, WIDTH)),
        out_shape=jax.ShapeDtypeStruct((16, 32, WIDTH), jnp.bfloat16),
        scratch_shapes=[
            pltpu.VMEM((2 * ROWS, WIDTH), jnp.bfloat16),
            pltpu.VMEM((2 * ROWS, WIDTH), jnp.bfloat16),
            pltpu.VMEM((WIDTH, ROWS), jnp.bfloat16),
        ],
        compiler_params=pltpu.CompilerParams(vmem_limit_bytes=VMEM_LIMIT),
        cost_estimate=pl.CostEstimate(flops=20_000_000_000, bytes_accessed=20_000_000, transcendentals=6_400_000),
        name="far_tokens",
    )(xa, xb, xo, mod, wk, wvt, wo, qq, acc, top)


def temporal_kernel(mid_ref, mod_ref, w_ref, wo_ref, out_ref, qkv_ref, att_ref):
    rows = 512
    x = mid_ref[...].reshape(rows, WIDTH)
    xn = modulate(x, mod_ref[3:4, :], mod_ref[4:5, :])
    for j in range(3):
        cols = slice(j * WIDTH, (j + 1) * WIDTH)
        part = jnp.dot(xn, w_ref[:, cols], preferred_element_type=jnp.float32)
        if j == 0:
            part = part * QSCALE
        qkv_ref[:, cols] = part
    lane = lax.broadcasted_iota(jnp.int32, (1, 256), 1)
    key_token = lax.broadcasted_iota(jnp.int32, (128, 256), 1) % 8
    query_token = lax.broadcasted_iota(jnp.int32, (128, 256), 0) % 8
    same = key_token == query_token
    groups = qkv_ref[...].reshape(16, 4, 8, 3 * WIDTH)
    for g in range(4):
        block = groups[:, g].reshape(128, 3 * WIDTH).astype(jnp.bfloat16)
        outs = []
        for p in range(PAIRS):
            win = slice(128 * p, 128 * p + 256)
            q = block[:, win]
            k = block[:, WIDTH + 128 * p : WIDTH + 128 * p + 256]
            v = block[:, 2 * WIDTH + 128 * p : 2 * WIDTH + 128 * p + 256]
            head_a = (lane >= 16 * p) & (lane < 16 * p + 72)
            head_b = (lane >= 16 * p + 72) & (lane < 16 * p + 144)
            zero = jnp.zeros_like(k)
            kk = jnp.concatenate([jnp.where(head_a, k, zero), jnp.where(head_b, k, zero)], axis=0)
            scores = lax.dot_general(q, kk, NT, preferred_element_type=jnp.float32)
            scores = jnp.where(same, scores, -1e30)
            top_a = jnp.max(scores[:, :128], axis=1, keepdims=True)
            top_b = jnp.max(scores[:, 128:], axis=1, keepdims=True)
            wa = jnp.where(same[:, :128], jnp.exp2(scores[:, :128] - top_a), 0.0)
            wb = jnp.where(same[:, 128:], jnp.exp2(scores[:, 128:] - top_b), 0.0)
            sum_a = jnp.sum(wa, axis=1, keepdims=True)
            sum_b = jnp.sum(wb, axis=1, keepdims=True)
            ww = jnp.concatenate([wa, wb], axis=1).astype(jnp.bfloat16)
            vv = jnp.concatenate([jnp.where(head_a, v, zero), jnp.where(head_b, v, zero)], axis=0)
            total = jnp.dot(ww, vv, preferred_element_type=jnp.float32)
            outs.append(jnp.where(head_a, total / sum_a, total / sum_b))
        tiles = []
        for t in range(9):
            left = outs[t][:, :128] if t < PAIRS else None
            right = outs[t - 1][:, 128:] if t > 0 else None
            if left is None:
                tiles.append(right)
            elif right is None:
                tiles.append(left)
            else:
                tiles.append(jnp.where(lane[:, :128] < 16 * t, right, left))
        merged = jnp.concatenate(tiles, axis=1).astype(jnp.bfloat16)
        att_ref[g * 128 : g * 128 + 128, :] = merged
    projected = jnp.dot(att_ref[...], wo_ref[...], preferred_element_type=jnp.float32)
    for g in range(4):
        piece = projected[g * 128 : g * 128 + 128].reshape(16, 8, WIDTH)
        rest = mid_ref[...].astype(jnp.float32)[:, 8 * g : 8 * g + 8, :]
        qkv_ref[:, 0:WIDTH].reshape(16, 32, WIDTH)
        done = rest + mod_ref[5:6, :][None] * piece
        qkv_ref[g * 128 : g * 128 + 128, 0:WIDTH] = done.reshape(128, WIDTH)
    final = qkv_ref[:, 0:WIDTH].reshape(4, 16, 8, WIDTH)
    for f in range(16):
        out_ref[f] = jnp.concatenate([final[g, f] for g in range(4)], axis=0).astype(jnp.bfloat16)


def temporal(mid, mod, w, wo):
    return pl.pallas_call(
        temporal_kernel,
        out_shape=jax.ShapeDtypeStruct((16, 32, WIDTH), jnp.bfloat16),
        in_specs=[pl.BlockSpec(memory_space=pltpu.VMEM)] * 4,
        out_specs=pl.BlockSpec(memory_space=pltpu.VMEM),
        scratch_shapes=[pltpu.VMEM((512, 3 * WIDTH), jnp.float32), pltpu.VMEM((512, WIDTH), jnp.bfloat16)],
        compiler_params=pltpu.CompilerParams(vmem_limit_bytes=VMEM_LIMIT),
        cost_estimate=pl.CostEstimate(flops=6_000_000_000, bytes_accessed=14_000_000, transcendentals=1_000_000),
        name="temporal_block",
    )(mid, mod, w, wo)


def local(clip, modulation, w_qkv_s, w_out_s, w_qkv_t, w_out_t):
    own = clip[0]
    swap_chip = [(0, 2), (1, 3), (2, 0), (3, 1)]
    swap_core = [(0, 1), (1, 0), (2, 3), (3, 2)]
    there = lax.ppermute(own, "head", swap_chip)
    peer = lax.ppermute(own, "head", swap_core)
    wk = w_qkv_s[:, WIDTH : 2 * WIDTH]
    wqt = w_qkv_s[:, :WIDTH].T
    wvt = w_qkv_s[:, 2 * WIDTH :].T
    qq, acc, top = near(own, peer, modulation, wk, wqt, wvt)
    there_peer = lax.ppermute(there, "head", swap_core)
    middle = far(there, there_peer, own, modulation, wk, wvt, w_out_s, qq, acc, top)
    block = lax.all_to_all(middle, "tm", split_axis=0, concat_axis=0, tiled=True)
    done = temporal(block, modulation, w_qkv_t, w_out_t)
    back = lax.all_to_all(done, "tm", split_axis=0, concat_axis=0, tiled=True)
    return back[:, :28, :].reshape(1, ROWS, WIDTH)


def solution(mesh):
    placed = (P(("dp", "tm"), "head", None), P("dp", None), P(), P(), P(), P())
    return jax.shard_map(
        local, mesh=mesh, in_specs=placed, out_specs=P(("dp", "tm"), "head", None), check_vma=False
    )
```

time: 317 us -> 153 us (0.48)
  Pallas kernels: 0 us -> 73.6 us
  local copies, waits for them, and re-layouts: 88.2 us -> 15.7 us
  matrix products: 58.3 us -> 0 us
  blocking collectives: 92.7 us -> 49.6 us
  waiting for transfers between devices: 42.5 us -> 10.2 us
  other arithmetic: 28.3 us -> 0 us
    pallas_call x0 -> x3, Pallas kernels: none -> 73.6 us  [the longest x1 27.3 us: far(): pl.pallas_call(functools.partial(far_kernel, tile), grid=(PAIRS,), in_spe...]
    dot_general x14 -> x0, matrix products: 58.3 us -> none  [the longest x5 18.1 us: attend_core(): jnp.einsum('nqk,nke->nqe', rounded, values, preferred_element_type=jnp.fl...]
    all_to_all x3 -> x2, blocking collectives: 92.7 us -> 49.6 us  [the longest x1 27.5 us: local(): lax.all_to_all(middle, 'tm', split_axis=0, concat_axis=0, tiled=True)]
    all_to_all x1 -> x0, waiting for transfers between devices: 42.5 us -> none  [local(): lax.all_to_all(grouped, 'head', split_axis=3, concat_axis=1, tiled=True)]
    reshape x7 -> x1, local copies, waits for them, and re-layouts: 36.6 us -> 1.06 us  [local(): return back[:, :28, :].reshape(1, ROWS, WIDTH)]
    all_to_all x5 -> x0, local copies, waits for them, and re-layouts: 20.3 us -> none  [the longest x3 11.3 us: local(): lax.all_to_all(attended, 'head', split_axis=1, concat_axis=2, tiled=True)]
    unnamed x1 -> x0, other arithmetic: 13.6 us -> none
    reduce_sum x8 -> x0, other arithmetic: 13.5 us -> none  [the longest x5 9.96 us: attend_core(): row_total = jnp.sum(weights, axis=-1, keepdims=True)]
  transfers between devices with their start and end apart: 1 -> 3, of which waited for: 1 -> 1; matrix products, arithmetic and copies ran while one was open for 0% -> 9% of each run, Pallas kernels for 0% -> 16%
where the time goes in v1:
time: 153 us; the launch traced here: 152 us
  Pallas kernels  73.6 us (48%)
  blocking collectives  49.6 us (32%)
  local copies, waits for them, and re-layouts  15.7 us (10%)
  waiting for transfers between devices  10.2 us (7%)
  starting transfers between devices  3.11 us (2%)
    all_to_all x1, blocking collectives, local(): lax.all_to_all(middle, 'tm', split_axis=0, concat_axis=0, tiled=True)  27.5 us
    pallas_call x1, Pallas kernels, far(): pl.pallas_call(functools.partial(far_kernel, tile), grid=(PAIRS,), in_spe...  27.3 us
    pallas_call x1, Pallas kernels, near(): pl.pallas_call(functools.partial(near_kernel, tile), grid=(PAIRS,), in_sp...  25.1 us
    all_to_all x1, blocking collectives, local(): back = lax.all_to_all(done, 'tm', split_axis=0, concat_axis=0, tiled=True)  22.1 us
    pallas_call x1, Pallas kernels, temporal(): pl.pallas_call(temporal_kernel, out_shape=jax.ShapeDtypeStruct((16, 32, W...  21.3 us
    ppermute x1, waiting for transfers between devices, local(): there = lax.ppermute(own, 'head', swap_chip)  10.2 us
    unnamed x4, local copies, waits for them, and re-layouts  9.49 us
    slice x1, local copies, waits for them, and re-layouts, local(): wqt = w_qkv_s[:, :WIDTH].T  5.17 us
  transfers between devices with their start and end apart: 3, of which 1 were waited for; matrix products, arithmetic and copies ran while one was open for 9% of the time, Pallas kernels for 16%

profile of v1, /device:TPU:0, one launch (start us, length us, event | category | flops | bytes accessed | tf_op | source)
XLA Modules:
  0.0 152.3 jit_solution(13856083730958721121)
XLA Ops:
  0.0 0.0 collective-permute-start.2
  0.0 3.1 %collective-permute-start = (bf16[448,1152]{1,0:T(8,128)(2,1)}, bf16[448,1152]{1,0:T(8,128)(2,1)}, u32[]{:S(2)}, u32[]{:S(2)}) collective-permute-start(bf16[448,1152]{1,0:T(8,128)(2,1)} %bitcast.9), channel_id=1, source_target_pairs={{0,2},{1,3},{2,0},{3,1},{4,6},{5,7},{6,4},{7,5},{8,10},{9,11},{10,... | collective-permute-start | bytes 3096584 | tf_op jit(solution)/shard_map/ppermute | solution.py:271
  3.1 5.2 %fusion = (bf16[1152,1152]{1,0:T(8,128)(2,1)S(1)}, bf16[1152,1152]{1,0:T(8,128)(2,1)}, bf16[1152,1152]{1,0:T(8,128)(2,1)}) fusion(bf16[1152,3456]{1,0:T(8,128)(2,1)} %param.8), kind=kLoop, calls=%fused_computation | loop fusion | bytes 15925248 | tf_op jit(solution)/shard_map/slice | solution.py:274
  8.3 5.2 %copy.11 = bf16[1152,1152]{0,1:T(8,128)(2,1)} copy(bf16[1152,1152]{1,0:T(8,128)(2,1)} %get-tuple-element.12) | data formatting | bytes 5308416
  13.5 3.3 %copy.12 = bf16[1152,1152]{0,1:T(8,128)(2,1)} copy(bf16[1152,1152]{1,0:T(8,128)(2,1)S(1)} %get-tuple-element.11) | data formatting | bytes 5308416
  16.8 10.2 %collective-permute-done.xa_ref = bf16[448,1152]{1,0:T(8,128)(2,1)} collective-permute-done((bf16[448,1152]{1,0:T(8,128)(2,1)}, bf16[448,1152]{1,0:T(8,128)(2,1)}, u32[]{:S(2)}, u32[]{:S(2)}) %collective-permute-start) | collective-permute-done | bytes 1032224 | tf_op jit(solution)/shard_map/ppermute | solution.py:271
  27.0 0.0 collective-permute-start.1
  27.0 0.0 collective-permute-done.2.xp_ref
  27.1 25.1 %near_tokens.1 = (bf16[8,256,896]{2,1,0:T(8,128)(2,1)}, f32[8,80,896]{2,1,0:T(8,128)}, f32[8,8,896]{2,1,0:T(8,128)}) custom-call(bf16[448,1152]{1,0:T(8,128)(2,1)} %bitcast.10, bf16[448,1152]{1,0:T(8,128)(2,1)} %collective-permute-done.2.xp_ref, f32[6,1152]{1,0:T(8,128)} %mod_ref.5, bf16[1152,1152]{1,0:T(8,128)(2,1)} %get-tuple-element.13.wk_ref, ...), custom_call_target="tpu_custom_call" | custom-call | flops 20000000000 | bytes 20000000 | tf_op jit(solution)/shard_map/near_tokens/pallas_call | solution.py:134
  52.1 0.0 collective-permute-done.1.xb_ref
  52.1 0.0 copy-start
  52.1 1.0 copy-done
  53.1 27.3 %far_tokens.1 = bf16[16,32,1152]{2,1,0:T(8,128)(2,1)} custom-call(bf16[448,1152]{1,0:T(8,128)(2,1)} %collective-permute-done.xa_ref, bf16[448,1152]{1,0:T(8,128)(2,1)} %copy-done, bf16[448,1152]{1,0:T(8,128)(2,1)} %bitcast.11, f32[6,1152]{1,0:T(8,128)} %mod_ref.5, bf16[1152,1152]{1,0:T(8,128)(2,1)} %get-tuple-element.13.wk_ref, bf16[1152,1152]{1,0:T(8,128)(2,1)} %bitcast.6, ...), custom_call_target="tpu_custom_call" | custom-call | flops 20000000000 | bytes 20000000 | tf_op jit(solution)/shard_map/far_tokens/pallas_call | solution.py:163
  80.3 27.5 %all_to_all.10.mid_ref = bf16[16,32,1152]{2,1,0:T(8,128)(2,1)} all-to-all(bf16[16,32,1152]{2,1,0:T(8,128)(2,1)} %far_tokens.1), channel_id=1, replica_groups=mesh['dp'=2,'tm'=16,'head'=4] {'tm'}, dimensions={0} | all-to-all | bytes 2359296 | tf_op jit(solution)/shard_map/all_to_all | solution.py:279
  107.9 21.3 %temporal_block.1 = bf16[16,32,1152]{2,1,0:T(8,128)(2,1)} custom-call(bf16[16,32,1152]{2,1,0:T(8,128)(2,1)} %all_to_all.10.mid_ref, f32[6,1152]{1,0:T(8,128)} %mod_ref.5, bf16[1152,3456]{1,0:T(8,128)(2,1)} %w_ref.1, bf16[1152,1152]{1,0:T(8,128)(2,1)} %wo_ref.3), custom_call_target="tpu_custom_call" | custom-call | flops 6000000000 | bytes 14000000 | tf_op jit(solution)/shard_map/temporal_block/pallas_call | solution.py:255
  129.1 22.1 %all_to_all.11 = bf16[16,32,1152]{2,1,0:T(8,128)(2,1)S(1)} all-to-all(bf16[16,32,1152]{2,1,0:T(8,128)(2,1)} %temporal_block.1), channel_id=1, replica_groups=mesh['dp'=2,'tm'=16,'head'=4] {'tm'}, dimensions={0} | all-to-all | bytes 2359296 | tf_op jit(solution)/shard_map/all_to_all | solution.py:281
  151.2 1.1 reshape.3
Async XLA Ops:
  0.0 27.1 %collective-permute-start.2 = (bf16[448,1152]{1,0:T(8,128)(2,1)}, bf16[448,1152]{1,0:T(8,128)(2,1)}, u32[]{:S(2)}, u32[]{:S(2)}) collective-permute-start(bf16[448,1152]{1,0:T(8,128)(2,1)} %bitcast.8), channel_id=1, source_target_pairs={{0,1},{1,0},{2,3},{3,2},{4,5},{5,4},{6,7},{7,6},{8,9},{9,8},{10,11... | collective-permute-start | bytes 3096584 | tf_op jit(solution)/shard_map/ppermute | solution.py:272
  0.0 27.0 %collective-permute-start = (bf16[448,1152]{1,0:T(8,128)(2,1)}, bf16[448,1152]{1,0:T(8,128)(2,1)}, u32[]{:S(2)}, u32[]{:S(2)}) collective-permute-start(bf16[448,1152]{1,0:T(8,128)(2,1)} %bitcast.9), channel_id=1, source_target_pairs={{0,2},{1,3},{2,0},{3,1},{4,6},{5,7},{6,4},{7,5},{8,10},{9,11},{10,... | collective-permute-start | bytes 3096584 | tf_op jit(solution)/shard_map/ppermute | solution.py:271
  27.0 25.1 %collective-permute-start.1 = (bf16[448,1152]{1,0:T(8,128)(2,1)}, bf16[448,1152]{1,0:T(8,128)(2,1)S(1)}, u32[]{:S(2)}, u32[]{:S(2)}) collective-permute-start(bf16[448,1152]{1,0:T(8,128)(2,1)} %collective-permute-done.xa_ref), channel_id=1, source_target_pairs={{0,1},{1,0},{2,3},{3,2},{4,5},{5,4},{6,7},{7,6},{8,9},{9,8},{10,11... | collective-permute-start | bytes 3096584 | tf_op jit(solution)/shard_map/ppermute | solution.py:277
  52.1 1.0 copy-start

commit v2 on v0

v2 whole, which is shorter than its diff:
```python
import math

import jax
import jax.numpy as jnp
from jax import lax
from jax.experimental import pallas as pl
from jax.experimental.pallas import tpu as pltpu
from jax.sharding import PartitionSpec as P

HEADS = 16
HEAD_DIM = 72
WIDTH = 1152
ROWS = 448
LANES = 896
WINDOW = 640
HALF_COLS = 576
AUG = 80
PADDED = 512
TILE = 512
QSCALE = math.log2(math.e) / math.sqrt(HEAD_DIM)
NT = (((1,), (1,)), ((), ()))
TN = (((0,), (0,)), ((), ()))
BF16 = jnp.bfloat16
F32 = jnp.float32
VMEM = pl.BlockSpec(memory_space=pltpu.VMEM)
SMEM = pl.BlockSpec(memory_space=pltpu.SMEM)
HBM = pl.BlockSpec(memory_space=pl.ANY)


def params():
    return pltpu.CompilerParams(vmem_limit_bytes=48 * 1024 * 1024)


def modulate(values, shift_vec, scale_vec):
    values = values.astype(F32)
    average = jnp.mean(values, axis=-1, keepdims=True)
    centred = values - average
    variance = jnp.mean(centred * centred, axis=-1, keepdims=True)
    normed = centred * lax.rsqrt(variance + 1e-06)
    return (normed * (1.0 + scale_vec) + shift_vec).astype(BF16)


def window_copies(w_hbm, w_ref, sems, core, thirds):
    copies = []
    for i, third in enumerate(thirds):
        start = pl.multiple_of(third * WIDTH + core * 512, 128)
        copies.append(
            pltpu.make_async_copy(
                w_hbm.at[:, pl.ds(start, WINDOW)], w_ref.at[:, i * WINDOW : (i + 1) * WINDOW], sems.at[i]
            )
        )
    return copies


def head_window(head, core):
    offset = head * HEAD_DIM + core * 64
    start = pl.multiple_of(jnp.minimum(offset // 128, 3) * 128, 128)
    return offset, start, offset - start


def attend_head(head, core, q_ref, keys_values, old):
    offset, start, inside = head_window(head, core)
    lane = lax.broadcasted_iota(jnp.int32, (1, 256), 1)
    mine = (lane >= inside) & (lane < inside + HEAD_DIM)
    queries = jnp.where(mine, q_ref[:, pl.ds(start, 256)], jnp.zeros((), BF16))
    keys, values = [], []
    for k_ref, vt_ref in keys_values:
        keys.append(k_ref[:, pl.ds(start, 256)])
        count = k_ref.shape[0]
        first = lax.broadcasted_iota(jnp.int32, (AUG - HEAD_DIM, count), 0) == 0
        vt = vt_ref[pl.ds(pl.multiple_of(offset, 8), HEAD_DIM), :]
        values.append(jnp.concatenate([vt, jnp.where(first, 1.0, 0.0)], axis=0).astype(BF16))
    starts = list(range(0, LANES, TILE))

    def score(s):
        part = queries[s : min(s + TILE, LANES)]
        return [lax.dot_general(k, part, NT, preferred_element_type=F32) for k in keys]

    out = []
    ahead = score(starts[0])
    for i, s in enumerate(starts):
        scores = ahead
        if i + 1 < len(starts):
            ahead = score(starts[i + 1])
        top = jnp.max(scores[0], axis=0, keepdims=True)
        for more in scores[1:]:
            top = jnp.maximum(top, jnp.max(more, axis=0, keepdims=True))
        total = None
        if old is not None:
            acc_ref, top_ref = old
            lanes = slice(s, s + scores[0].shape[1])
            before = top_ref[head, 0:1, lanes]
            top = jnp.maximum(top, before)
            total = acc_ref[head, :, lanes] * jnp.exp2(before - top)
        for value, part in zip(values, scores):
            term = jnp.dot(value, jnp.exp2(part - top).astype(BF16), preferred_element_type=F32)
            total = term if total is None else total + term
        out.append((s, total, top))
    return out


def near_kernel(core_ref, xo_ref, xp_ref, mod_ref, w_hbm, q_ref, acc_ref, top_ref, xn_ref, w_ref, k_ref, vt_ref, sems):
    core = core_ref[0]
    copies = window_copies(w_hbm, w_ref, sems, core, (0, 1, 2))
    for copy in copies:
        copy.start()
    xn_ref[0:ROWS, :] = modulate(xo_ref[...], mod_ref[0:1, :], mod_ref[1:2, :])
    xn_ref[ROWS:, :] = modulate(xp_ref[...], mod_ref[0:1, :], mod_ref[1:2, :])
    for copy in copies:
        copy.wait()
    packed = jnp.dot(xn_ref[...], w_ref[...], preferred_element_type=F32)
    q_ref[...] = (packed[:, :WINDOW] * QSCALE).astype(BF16)
    k_ref[...] = packed[:, WINDOW : 2 * WINDOW].astype(BF16)
    vt_ref[...] = packed[:, 2 * WINDOW :].T

    def pair(p, carry):
        for h in range(2):
            head = 2 * p + h
            for s, total, top in attend_head(head, core, q_ref, ((k_ref, vt_ref),), None):
                width = total.shape[1]
                acc_ref[head, :, s : s + width] = total
                top_ref[head, :, s : s + width] = jnp.broadcast_to(top, (8, width))
        return carry

    lax.fori_loop(0, 4, pair, 0)


def near(core, xo, xp, mod, w):
    return pl.pallas_call(
        near_kernel,
        in_specs=[SMEM, VMEM, VMEM, VMEM, HBM],
        out_specs=[VMEM] * 3,
        out_shape=[
            jax.ShapeDtypeStruct((LANES, WINDOW), BF16),
            jax.ShapeDtypeStruct((8, AUG, LANES), F32),
            jax.ShapeDtypeStruct((8, 8, LANES), F32),
        ],
        scratch_shapes=[
            pltpu.VMEM((LANES, WIDTH), BF16),
            pltpu.VMEM((WIDTH, 3 * WINDOW), BF16),
            pltpu.VMEM((LANES, WINDOW), BF16),
            pltpu.VMEM((WINDOW, LANES), F32),
            pltpu.SemaphoreType.DMA((3,)),
        ],
        compiler_params=params(),
        cost_estimate=pl.CostEstimate(flops=20_000_000_000, bytes_accessed=10_000_000, transcendentals=6_400_000),
        name="near_tokens",
    )(core, xo, xp, mod, w)


def project_kernel(core_ref, x_ref, mod_ref, w_hbm, k_ref, vt_ref, w_ref, sems):
    copies = window_copies(w_hbm, w_ref, sems, core_ref[0], (1, 2))
    for copy in copies:
        copy.start()
    xn = modulate(x_ref[...], mod_ref[0:1, :], mod_ref[1:2, :])
    for copy in copies:
        copy.wait()
    packed = jnp.dot(xn, w_ref[...], preferred_element_type=F32)
    k_ref[...] = packed[:, :WINDOW].astype(BF16)
    vt_ref[...] = packed[:, WINDOW:].T


def project(core, x, mod, w):
    return pl.pallas_call(
        project_kernel,
        in_specs=[SMEM, VMEM, VMEM, HBM],
        out_specs=[VMEM] * 2,
        out_shape=[jax.ShapeDtypeStruct((ROWS, WINDOW), BF16), jax.ShapeDtypeStruct((WINDOW, ROWS), F32)],
        scratch_shapes=[pltpu.VMEM((WIDTH, 2 * WINDOW), BF16), pltpu.SemaphoreType.DMA((2,))],
        compiler_params=params(),
        cost_estimate=pl.CostEstimate(flops=2_000_000_000, bytes_accessed=6_000_000, transcendentals=0),
        name="far_keys",
    )(core, x, mod, w)


def far_kernel(
    core_ref, x_ref, mod_ref, w_hbm, k1_ref, vt1_ref, q_ref, acc_ref, top_ref, own_ref, peer_ref, w_ref, k_ref, vt_ref, sems
):
    core = core_ref[0]
    project_kernel(core_ref, x_ref, mod_ref, w_hbm, k_ref, vt_ref, w_ref, sems)

    def pair(p, carry):
        halves = []
        for h in range(2):
            parts = attend_head(
                2 * p + h, core, q_ref, ((k1_ref, vt1_ref), (k_ref, vt_ref)), (acc_ref, top_ref)
            )
            halves.append(
                jnp.concatenate([t[:HEAD_DIM] / t[HEAD_DIM : HEAD_DIM + 1] for _, t, _ in parts], axis=1)
            )
        both = jnp.concatenate(halves, axis=0)
        rows = pl.ds(pl.multiple_of(p * 2 * HEAD_DIM, 16), 2 * HEAD_DIM)
        own_ref[rows, :] = both[:, :ROWS].astype(BF16)
        peer_ref[rows, :] = jnp.concatenate(
            [both[:, ROWS:], jnp.zeros((2 * HEAD_DIM, PADDED - ROWS), F32)], axis=1
        ).astype(BF16)
        return carry

    lax.fori_loop(0, 4, pair, 0)


def far(core, x, mod, w, k1, vt1, q, acc, top):
    return pl.pallas_call(
        far_kernel,
        in_specs=[SMEM, VMEM, VMEM, HBM] + [VMEM] * 5,
        out_specs=[VMEM] * 2,
        out_shape=[jax.ShapeDtypeStruct((HALF_COLS, ROWS), BF16), jax.ShapeDtypeStruct((HALF_COLS, PADDED), BF16)],
        scratch_shapes=[
            pltpu.VMEM((WIDTH, 2 * WINDOW), BF16),
            pltpu.VMEM((ROWS, WINDOW), BF16),
            pltpu.VMEM((WINDOW, ROWS), F32),
            pltpu.SemaphoreType.DMA((2,)),
        ],
        compiler_params=params(),
        cost_estimate=pl.CostEstimate(flops=18_000_000_000, bytes_accessed=10_000_000, transcendentals=6_400_000),
        name="far_tokens",
    )(core, x, mod, w, k1, vt1, q, acc, top)


def join_kernel(core_ref, mine_ref, other_ref, x_ref, mod_ref, wo_ref, out_ref, att_ref):
    core = core_ref[0]
    att_ref[pl.ds(pl.multiple_of(core * HALF_COLS, 16), HALF_COLS), :] = mine_ref[...]
    att_ref[pl.ds(pl.multiple_of((1 - core) * HALF_COLS, 16), HALF_COLS), :] = other_ref[:, :ROWS]
    projected = lax.dot_general(att_ref[...], wo_ref[...], TN, preferred_element_type=F32)
    middle = x_ref[...].astype(F32) + mod_ref[2:3, :] * projected
    for d in range(16):
        piece = jnp.concatenate([middle[28 * d : 28 * d + 28], jnp.zeros((4, WIDTH), F32)], axis=0)
        out_ref[d] = piece.astype(BF16)


def join(core, mine, other, x, mod, wo):
    return pl.pallas_call(
        join_kernel,
        in_specs=[SMEM] + [VMEM] * 5,
        out_specs=VMEM,
        out_shape=jax.ShapeDtypeStruct((16, 32, WIDTH), BF16),
        scratch_shapes=[pltpu.VMEM((WIDTH, ROWS), BF16)],
        compiler_params=params(),
        cost_estimate=pl.CostEstimate(flops=1_200_000_000, bytes_accessed=6_000_000, transcendentals=0),
        name="spatial_out",
    )(core, mine, other, x, mod, wo)


def temporal_kernel(mid_ref, mod_ref, w_hbm, wo_hbm, out_ref, x_ref, w_ref, wo_ref, q_ref, k_ref, vt_ref, att_ref, sems):
    copies = [
        pltpu.make_async_copy(w_hbm.at[:, i * WIDTH : (i + 1) * WIDTH], w_ref.at[:, i * WIDTH : (i + 1) * WIDTH], sems.at[i])
        for i in range(3)
    ]
    copies.append(pltpu.make_async_copy(wo_hbm, wo_ref, sems.at[3]))
    for copy in copies:
        copy.start()
    for g in range(4):
        for f in range(16):
            x_ref[(g * 16 + f) * 8 : (g * 16 + f + 1) * 8, :] = mid_ref[f].astype(F32)[8 * g : 8 * g + 8]
    xn = modulate(x_ref[...], mod_ref[3:4, :], mod_ref[4:5, :])
    for copy in copies[:3]:
        copy.wait()
    packed = jnp.dot(xn, w_ref[...], preferred_element_type=F32)
    q_ref[...] = (packed[:, :WIDTH] * QSCALE).astype(BF16)
    k_ref[...] = packed[:, WIDTH : 2 * WIDTH].astype(BF16)
    vt_ref[...] = packed[:, 2 * WIDTH :].T
    lane = lax.broadcasted_iota(jnp.int32, (1, 256), 1)
    same = lax.broadcasted_iota(jnp.int32, (128, 256), 0) % 8 == lax.broadcasted_iota(jnp.int32, (128, 256), 1) % 8
    tail = jnp.where(lax.broadcasted_iota(jnp.int32, (AUG - HEAD_DIM, 128), 0) == 0, 1.0, 0.0)

    for g in range(4):
        rows = slice(g * 128, (g + 1) * 128)
        for p in range(8):
            inside = 16 * p
            window = slice(128 * p, 128 * p + 256)
            q = q_ref[rows, window]
            none = jnp.zeros((), BF16)
            first = jnp.where((lane >= inside) & (lane < inside + HEAD_DIM), q, none)
            second = jnp.where((lane >= inside + HEAD_DIM) & (lane < inside + 2 * HEAD_DIM), q, none)
            queries = jnp.concatenate([first, second], axis=0)
            scores = lax.dot_general(k_ref[rows, window], queries, NT, preferred_element_type=F32)
            scores = jnp.where(same, scores, -1e30)
            top = jnp.max(scores, axis=0, keepdims=True)
            weights = jnp.exp2(scores - top).astype(BF16)
            at = 2 * HEAD_DIM * p
            values = jnp.concatenate(
                [vt_ref[at : at + HEAD_DIM, rows], tail, vt_ref[at + HEAD_DIM : at + 2 * HEAD_DIM, rows], tail], axis=0
            ).astype(BF16)
            total = jnp.dot(values, weights, preferred_element_type=F32)
            a = total[:HEAD_DIM, :128] / total[HEAD_DIM : HEAD_DIM + 1, :128]
            b = total[AUG : AUG + HEAD_DIM, 128:] / total[AUG + HEAD_DIM : AUG + HEAD_DIM + 1, 128:]
            att_ref[at : at + 2 * HEAD_DIM, rows] = jnp.concatenate([a, b], axis=0).astype(BF16)
    copies[3].wait()
    projected = lax.dot_general(att_ref[...], wo_ref[...], TN, preferred_element_type=F32)
    x_ref[...] = x_ref[...] + mod_ref[5:6, :] * projected
    for f in range(16):
        pieces = [x_ref[(g * 16 + f) * 8 : (g * 16 + f + 1) * 8, :] for g in range(4)]
        out_ref[f] = jnp.concatenate(pieces, axis=0).astype(BF16)


def temporal(mid, mod, w, wo):
    return pl.pallas_call(
        temporal_kernel,
        in_specs=[VMEM, VMEM, HBM, HBM],
        out_specs=VMEM,
        out_shape=jax.ShapeDtypeStruct((16, 32, WIDTH), BF16),
        scratch_shapes=[
            pltpu.VMEM((512, WIDTH), F32),
            pltpu.VMEM((WIDTH, 3 * WIDTH), BF16),
            pltpu.VMEM((WIDTH, WIDTH), BF16),
            pltpu.VMEM((512, WIDTH), BF16),
            pltpu.VMEM((512, WIDTH), BF16),
            pltpu.VMEM((WIDTH, 512), F32),
            pltpu.VMEM((WIDTH, 512), BF16),
            pltpu.SemaphoreType.DMA((4,)),
        ],
        compiler_params=params(),
        cost_estimate=pl.CostEstimate(flops=6_000_000_000, bytes_accessed=14_000_000, transcendentals=1_000_000),
        name="temporal_block",
    )(mid, mod, w, wo)


def local(clip, modulation, w_qkv_s, w_out_s, w_qkv_t, w_out_t):
    own = clip[0]
    core = (lax.axis_index("head") % 2).astype(jnp.int32).reshape(1)
    swap_chip = [(0, 2), (1, 3), (2, 0), (3, 1)]
    swap_core = [(0, 1), (1, 0), (2, 3), (3, 2)]
    peer = lax.ppermute(own, "head", swap_core)
    there = lax.ppermute(own, "head", swap_chip)
    q, acc, top = near(core, own, peer, modulation, w_qkv_s)
    there, q = lax.optimization_barrier((there, q))
    k1, vt1 = project(core, there, modulation, w_qkv_s)
    there_peer = lax.ppermute(there, "head", swap_core)
    mine, theirs = far(core, there_peer, modulation, w_qkv_s, k1, vt1, q, acc, top)
    other = lax.ppermute(theirs, "head", swap_core)
    middle = join(core, mine, other, own, modulation, w_out_s)
    block = lax.all_to_all(middle, "tm", split_axis=0, concat_axis=0, tiled=True)
    done = temporal(block, modulation, w_qkv_t, w_out_t)
    back = lax.all_to_all(done, "tm", split_axis=0, concat_axis=0, tiled=True)
    return back[:, :28, :].reshape(1, ROWS, WIDTH)


def solution(mesh):
    placed = (P(("dp", "tm"), "head", None), P("dp", None), P(), P(), P(), P())
    return jax.shard_map(
        local, mesh=mesh, in_specs=placed, out_specs=P(("dp", "tm"), "head", None), check_vma=False
    )
```

time: 317 us -> 119 us (0.38)
  local copies, waits for them, and re-layouts: 88.2 us -> 3.1 us
  matrix products: 58.3 us -> 0 us
  Pallas kernels: 0 us -> 57.3 us
  blocking collectives: 92.7 us -> 48.3 us
  waiting for transfers between devices: 42.5 us -> 5.97 us
  other arithmetic: 28.3 us -> 0 us
    dot_general x14 -> x0, matrix products: 58.3 us -> none  [the longest x5 18.1 us: attend_core(): jnp.einsum('nqk,nke->nqe', rounded, values, preferred_element_type=jnp.fl...]
    pallas_call x0 -> x5, Pallas kernels: none -> 57.3 us  [the longest x1 18.6 us: temporal(): pl.pallas_call(temporal_kernel, in_specs=[VMEM, VMEM, HBM, HBM], out_spec...]
    all_to_all x3 -> x2, blocking collectives: 92.7 us -> 48.3 us  [the longest x1 27.1 us: local(): lax.all_to_all(middle, 'tm', split_axis=0, concat_axis=0, tiled=True)]
    all_to_all x1 -> x0, waiting for transfers between devices: 42.5 us -> none  [local(): lax.all_to_all(grouped, 'head', split_axis=3, concat_axis=1, tiled=True)]
    reshape x7 -> x1, local copies, waits for them, and re-layouts: 36.6 us -> 1.06 us  [local(): return back[:, :28, :].reshape(1, ROWS, WIDTH)]
    all_to_all x5 -> x0, local copies, waits for them, and re-layouts: 20.3 us -> none  [the longest x3 11.3 us: local(): lax.all_to_all(attended, 'head', split_axis=1, concat_axis=2, tiled=True)]
    unnamed x1 -> x0, other arithmetic: 13.6 us -> none
    reduce_sum x8 -> x0, other arithmetic: 13.5 us -> none  [the longest x5 9.96 us: attend_core(): row_total = jnp.sum(weights, axis=-1, keepdims=True)]
  transfers between devices with their start and end apart: 1 -> 4, of which waited for: 1 -> 2; matrix products, arithmetic and copies ran while one was open for 0% -> 0% of each run, Pallas kernels for 0% -> 18%
where the time goes in v2:
time: 119 us; the launch traced here: 118 us
  Pallas kernels  57.3 us (48%)
  blocking collectives  48.3 us (41%)
  waiting for transfers between devices  5.97 us (5%)
  starting transfers between devices  3.71 us (3%)
  local copies, waits for them, and re-layouts  3.1 us (3%)
    all_to_all x1, blocking collectives, local(): lax.all_to_all(middle, 'tm', split_axis=0, concat_axis=0, tiled=True)  27.1 us
    all_to_all x1, blocking collectives, local(): back = lax.all_to_all(done, 'tm', split_axis=0, concat_axis=0, tiled=True)  21.2 us
    pallas_call x1, Pallas kernels, temporal(): pl.pallas_call(temporal_kernel, in_specs=[VMEM, VMEM, HBM, HBM], out_spec...  18.6 us
    pallas_call x1, Pallas kernels, near(): pl.pallas_call(near_kernel, in_specs=[SMEM, VMEM, VMEM, VMEM, HBM], out_s...  17.5 us
    pallas_call x1, Pallas kernels, far(): pl.pallas_call(far_kernel, in_specs=[SMEM, VMEM, VMEM, HBM] + [VMEM] * 5,...  15.6 us
    ppermute x1, waiting for transfers between devices, local(): there = lax.ppermute(own, 'head', swap_chip)  4.34 us
    pallas_call x1, Pallas kernels, project(): pl.pallas_call(project_kernel, in_specs=[SMEM, VMEM, VMEM, HBM], out_spec...  3.86 us
    ppermute x1, starting transfers between devices, local(): there = lax.ppermute(own, 'head', swap_chip)  3.11 us
  transfers between devices with their start and end apart: 4, of which 2 were waited for; matrix products, arithmetic and copies ran while one was open for 0% of the time, Pallas kernels for 18%

profile of v2, /device:TPU:0, one launch (start us, length us, event | category | flops | bytes accessed | tf_op | source)
XLA Modules:
  0.0 118.5 jit_solution(1110153210981657758)
XLA Ops:
  0.0 0.0 collective-permute-start.1
  0.0 3.1 %collective-permute-start = (bf16[448,1152]{1,0:T(8,128)(2,1)}, bf16[448,1152]{1,0:T(8,128)(2,1)S(1)}, u32[]{:S(2)}, u32[]{:S(2)}) collective-permute-start(bf16[448,1152]{1,0:T(8,128)(2,1)} %bitcast.4), channel_id=1, source_target_pairs={{0,2},{1,3},{2,0},{3,1},{4,6},{5,7},{6,4},{7,5},{8,10},{9,11},{10,... | collective-permute-start | bytes 3096584 | tf_op jit(solution)/shard_map/ppermute | solution.py:324
  3.1 0.0 collective-permute-done.1.xp_ref
  3.1 0.0 copy-start.1
  3.1 1.2 %copy-done.1 = bf16[1,448,1152]{2,1,0:T(8,128)(2,1)S(1)} copy-done((bf16[1,448,1152]{2,1,0:T(8,128)(2,1)S(1)}, bf16[1,448,1152]{2,1,0:T(8,128)(2,1)}, u32[]{:S(2)}) %copy-start.1) | copy-done | bytes 1032216
  4.4 0.0 copy-start.3
  4.4 0.8 copy-done.3
  5.1 17.5 %near_tokens.1 = (bf16[896,640]{1,0:T(8,128)(2,1)S(1)}, f32[8,80,896]{2,1,0:T(8,128)S(1)}, f32[8,8,896]{2,1,0:T(8,128)S(1)}) custom-call(s32[1]{0:T(128)} %bitcast.core_ref, bf16[448,1152]{1,0:T(8,128)(2,1)S(1)} %bitcast.5, bf16[448,1152]{1,0:T(8,128)(2,1)S(1)} %collective-permute-done.1.xp_ref, f32[6,1152]{1,0:T(8,128)S(1)} %copy-done.3, ...), custom_call_target="tpu_custom_call" | custom-call | flops 20000000000 | bytes 10000000 | tf_op jit(solution)/shard_map/near_tokens/pallas_call | solution.py:129
  22.6 0.0 copy-start.6
  22.6 4.3 %collective-permute-done.x_ref = bf16[448,1152]{1,0:T(8,128)(2,1)S(1)} collective-permute-done((bf16[448,1152]{1,0:T(8,128)(2,1)}, bf16[448,1152]{1,0:T(8,128)(2,1)S(1)}, u32[]{:S(2)}, u32[]{:S(2)}) %collective-permute-start) | collective-permute-done | bytes 1032224 | tf_op jit(solution)/shard_map/ppermute | solution.py:324
  26.9 0.0 collective-permute-start.2
  26.9 3.9 %far_keys.1 = (bf16[448,640]{1,0:T(8,128)(2,1)S(1)}, f32[640,448]{1,0:T(8,128)S(1)}) custom-call(s32[1]{0:T(128)} %bitcast.core_ref, bf16[448,1152]{1,0:T(8,128)(2,1)S(1)} %collective-permute-done.x_ref, f32[6,1152]{1,0:T(8,128)S(1)} %copy-done.3, bf16[1152,3456]{1,0:T(8,128)(2,1)} %w_hbm.6), custom_call_target="tpu_custom_call" | custom-call | flops 2000000000 | bytes 6000000 | tf_op jit(solution)/shard_map/far_keys/pallas_call | solution.py:164
  30.8 0.0 copy-done.6
  30.8 0.0 collective-permute-done.2.x_ref
  30.8 0.0 copy-start
  30.8 0.0 copy-start.2
  30.9 15.6 %far_tokens.1 = (bf16[576,448]{1,0:T(8,128)(2,1)S(1)}, bf16[576,512]{1,0:T(8,128)(2,1)S(1)}) custom-call(s32[1]{0:T(128)} %bitcast.core_ref, bf16[448,1152]{1,0:T(8,128)(2,1)S(1)} %collective-permute-done.2.x_ref, f32[6,1152]{1,0:T(8,128)S(1)} %copy-done.3, bf16[1152,3456]{1,0:T(8,128)(2,1)} %w_hbm.6, bf16[448,640]{1,0:T(8,128)(2,1)S(1)} %get-tuple-element.16.k1_ref, ...), custom_call_target="tpu_custom_call" | custom-call | flops 17999998976 | bytes 10000000 | tf_op jit(solution)/shard_map/far_tokens/pallas_call | solution.py:203
  46.5 0.6 collective-permute-start.3
  47.1 1.6 %collective-permute-done.3.other_ref = bf16[576,512]{1,0:T(8,128)(2,1)S(1)} collective-permute-done((bf16[576,512]{1,0:T(8,128)(2,1)S(1)}, bf16[576,512]{1,0:T(8,128)(2,1)S(1)}, u32[]{:S(2)}, u32[]{:S(2)}) %collective-permute-start.3) | collective-permute-done | bytes 589856 | tf_op jit(solution)/shard_map/ppermute | solution.py:330
  48.7 0.0 copy-done
  48.7 0.0 copy-done.2
  48.7 0.0 copy-start.5
  48.7 1.8 %spatial_out.1 = bf16[16,32,1152]{2,1,0:T(8,128)(2,1)S(1)} custom-call(s32[1]{0:T(128)} %bitcast.core_ref, bf16[576,448]{1,0:T(8,128)(2,1)S(1)} %get-tuple-element.21.mine_ref, bf16[576,512]{1,0:T(8,128)(2,1)S(1)} %collective-permute-done.3.other_ref, bf16[448,1152]{1,0:T(8,128)(2,1)S(1)} %bitcast.6, f32[6,1152]{1,0:T(8,128)S(1)} %copy-done.3, ...), custom_call_target="tpu_custom_call" | custom-call | flops 1200000000 | bytes 6000000 | tf_op jit(solution)/shard_map/spatial_out/pallas_call | solution.py:232
  50.5 0.0 copy-start.4
  50.5 27.1 %all_to_all.10.mid_ref = bf16[16,32,1152]{2,1,0:T(8,128)(2,1)S(1)} all-to-all(bf16[16,32,1152]{2,1,0:T(8,128)(2,1)S(1)} %spatial_out.1), channel_id=1, replica_groups=mesh['dp'=2,'tm'=16,'head'=4] {'tm'}, dimensions={0} | all-to-all | bytes 2359296 | tf_op jit(solution)/shard_map/all_to_all | solution.py:332
  77.6 0.0 copy-done.5
  77.6 0.0 copy-done.4
  77.6 18.6 %temporal_block.1 = bf16[16,32,1152]{2,1,0:T(8,128)(2,1)S(1)} custom-call(bf16[16,32,1152]{2,1,0:T(8,128)(2,1)S(1)} %all_to_all.10.mid_ref, f32[6,1152]{1,0:T(8,128)S(1)} %copy-done.4, bf16[1152,3456]{1,0:T(8,128)(2,1)} %w_hbm.7, bf16[1152,1152]{1,0:T(8,128)(2,1)S(1)} %copy-done.5), custom_call_target="tpu_custom_call" | custom-call | flops 6000000000 | bytes 14000000 | tf_op jit(solution)/shard_map/temporal_block/pallas_call | solution.py:297
  96.2 21.2 %all_to_all.11 = bf16[16,32,1152]{2,1,0:T(8,128)(2,1)S(1)} all-to-all(bf16[16,32,1152]{2,1,0:T(8,128)(2,1)S(1)} %temporal_block.1), channel_id=1, replica_groups=mesh['dp'=2,'tm'=16,'head'=4] {'tm'}, dimensions={0} | all-to-all | bytes 2359296 | tf_op jit(solution)/shard_map/all_to_all | solution.py:334
  117.4 1.1 reshape.7
Async XLA Ops:
  0.0 3.1 %collective-permute-start.1 = (bf16[448,1152]{1,0:T(8,128)(2,1)}, bf16[448,1152]{1,0:T(8,128)(2,1)S(1)}, u32[]{:S(2)}, u32[]{:S(2)}) collective-permute-start(bf16[448,1152]{1,0:T(8,128)(2,1)} %bitcast.3), channel_id=1, source_target_pairs={{0,1},{1,0},{2,3},{3,2},{4,5},{5,4},{6,7},{7,6},{8,9},{9,8},{10,11... | collective-permute-start | bytes 3096584 | tf_op jit(solution)/shard_map/ppermute | solution.py:323
  0.0 26.9 %collective-permute-start = (bf16[448,1152]{1,0:T(8,128)(2,1)}, bf16[448,1152]{1,0:T(8,128)(2,1)S(1)}, u32[]{:S(2)}, u32[]{:S(2)}) collective-permute-start(bf16[448,1152]{1,0:T(8,128)(2,1)} %bitcast.4), channel_id=1, source_target_pairs={{0,2},{1,3},{2,0},{3,1},{4,6},{5,7},{6,4},{7,5},{8,10},{9,11},{10,... | collective-permute-start | bytes 3096584 | tf_op jit(solution)/shard_map/ppermute | solution.py:324
  3.1 1.2 %copy-start.1 = (bf16[1,448,1152]{2,1,0:T(8,128)(2,1)S(1)}, bf16[1,448,1152]{2,1,0:T(8,128)(2,1)}, u32[]{:S(2)}) copy-start(bf16[1,448,1152]{2,1,0:T(8,128)(2,1)} %param.6) | copy-start | bytes 3096580
  4.4 0.8 copy-start.3
  22.6 8.2 %copy-start.6 = (f32[8,80,896]{2,1,0:T(8,128)}, f32[8,80,896]{2,1,0:T(8,128)S(1)}, u32[]{:S(2)}) copy-start(f32[8,80,896]{2,1,0:T(8,128)S(1)} %get-tuple-element.19.acc_ref) | copy-start | bytes 6881284
  26.9 3.9 %collective-permute-start.2 = (bf16[448,1152]{1,0:T(8,128)(2,1)S(1)}, bf16[448,1152]{1,0:T(8,128)(2,1)S(1)}, u32[]{:S(2)}, u32[]{:S(2)}) collective-permute-start(bf16[448,1152]{1,0:T(8,128)(2,1)S(1)} %collective-permute-done.x_ref), channel_id=1, source_target_pairs={{0,1},{1,0},{2,3},{3,2},{4,5},{5,4},{6,7},{7,6},{8,9},{9,8},{10,11... | collective-permute-start | bytes 3096584 | tf_op jit(solution)/shard_map/ppermute | solution.py:328
  30.8 17.9 %copy-start = (bf16[1152,1152]{1,0:T(8,128)(2,1)S(1)}, bf16[1152,1152]{1,0:T(8,128)(2,1)}, u32[]{:S(2)}) copy-start(bf16[1152,1152]{1,0:T(8,128)(2,1)} %wo_ref.1) | copy-start | bytes 7962628
  30.8 17.9 %copy-start.2 = (bf16[1,448,1152]{2,1,0:T(8,128)(2,1)S(1)}, bf16[1,448,1152]{2,1,0:T(8,128)(2,1)}, u32[]{:S(2)}) copy-start(bf16[1,448,1152]{2,1,0:T(8,128)(2,1)} %param.6) | copy-start | bytes 3096580
  46.5 2.2 %collective-permute-start.3 = (bf16[576,512]{1,0:T(8,128)(2,1)S(1)}, bf16[576,512]{1,0:T(8,128)(2,1)S(1)}, u32[]{:S(2)}, u32[]{:S(2)}) collective-permute-start(bf16[576,512]{1,0:T(8,128)(2,1)S(1)} %get-tuple-element.22), channel_id=1, source_target_pairs={{0,1},{1,0},{2,3},{3,2},{4,5},{5,4},{6,7},{7,6},{8,9},{9,8},{10,11... | collective-permute-start | bytes 1769480 | tf_op jit(solution)/shard_map/ppermute | solution.py:330
  48.7 28.9 %copy-start.5 = (bf16[1152,1152]{1,0:T(8,128)(2,1)S(1)}, bf16[1152,1152]{1,0:T(8,128)(2,1)}, u32[]{:S(2)}) copy-start(bf16[1152,1152]{1,0:T(8,128)(2,1)} %wo_hbm.1) | copy-start | bytes 7962628
  50.5 27.1 %copy-start.4 = (f32[6,1152]{1,0:T(8,128)S(1)}, f32[6,1152]{1,0:T(8,128)}, u32[]{:S(2)}) copy-start(f32[6,1152]{1,0:T(8,128)} %mod_ref.9) | copy-start | bytes 82948

commit v3 on v2

--- a/solution.py
+++ b/solution.py
@@ -27,8 +27,8 @@
 HBM = pl.BlockSpec(memory_space=pl.ANY)
 
 
-def params():
-    return pltpu.CompilerParams(vmem_limit_bytes=48 * 1024 * 1024)
+def params(mebibytes):
+    return pltpu.CompilerParams(vmem_limit_bytes=mebibytes * 1024 * 1024)
 
 
 def modulate(values, shift_vec, scale_vec):
@@ -142,7 +142,7 @@
             pltpu.VMEM((WINDOW, LANES), F32),
             pltpu.SemaphoreType.DMA((3,)),
         ],
-        compiler_params=params(),
+        compiler_params=params(36),
         cost_estimate=pl.CostEstimate(flops=20_000_000_000, bytes_accessed=10_000_000, transcendentals=6_400_000),
         name="near_tokens",
     )(core, xo, xp, mod, w)
@@ -167,7 +167,7 @@
         out_specs=[VMEM] * 2,
         out_shape=[jax.ShapeDtypeStruct((ROWS, WINDOW), BF16), jax.ShapeDtypeStruct((WINDOW, ROWS), F32)],
         scratch_shapes=[pltpu.VMEM((WIDTH, 2 * WINDOW), BF16), pltpu.SemaphoreType.DMA((2,))],
-        compiler_params=params(),
+        compiler_params=params(16),
         cost_estimate=pl.CostEstimate(flops=2_000_000_000, bytes_accessed=6_000_000, transcendentals=0),
         name="far_keys",
     )(core, x, mod, w)
@@ -211,7 +211,7 @@
             pltpu.VMEM((WINDOW, ROWS), F32),
             pltpu.SemaphoreType.DMA((2,)),
         ],
-        compiler_params=params(),
+        compiler_params=params(36),
         cost_estimate=pl.CostEstimate(flops=18_000_000_000, bytes_accessed=10_000_000, transcendentals=6_400_000),
         name="far_tokens",
     )(core, x, mod, w, k1, vt1, q, acc, top)
@@ -235,81 +235,104 @@
         out_specs=VMEM,
         out_shape=jax.ShapeDtypeStruct((16, 32, WIDTH), BF16),
         scratch_shapes=[pltpu.VMEM((WIDTH, ROWS), BF16)],
-        compiler_params=params(),
+        compiler_params=params(14),
         cost_estimate=pl.CostEstimate(flops=1_200_000_000, bytes_accessed=6_000_000, transcendentals=0),
         name="spatial_out",
     )(core, mine, other, x, mod, wo)
 
 
-def temporal_kernel(mid_ref, mod_ref, w_hbm, wo_hbm, out_ref, x_ref, w_ref, wo_ref, q_ref, k_ref, vt_ref, att_ref, sems):
-    copies = [
-        pltpu.make_async_copy(w_hbm.at[:, i * WIDTH : (i + 1) * WIDTH], w_ref.at[:, i * WIDTH : (i + 1) * WIDTH], sems.at[i])
-        for i in range(3)
-    ]
-    copies.append(pltpu.make_async_copy(wo_hbm, wo_ref, sems.at[3]))
-    for copy in copies:
-        copy.start()
-    for g in range(4):
-        for f in range(16):
-            x_ref[(g * 16 + f) * 8 : (g * 16 + f + 1) * 8, :] = mid_ref[f].astype(F32)[8 * g : 8 * g + 8]
+def temporal_kernel(mid_ref, mod_ref, w_ref, wo_ref, out_ref, x_ref, q_ref, k_ref, vt_ref, att_ref):
+    for i in range(8):
+        lows = []
+        for f in (2 * i, 2 * i + 1):
+            frame = mid_ref[f].astype(F32)
+            for g in range(3):
+                x_ref[(g * 16 + f) * 8 : (g * 16 + f + 1) * 8, :] = frame[8 * g : 8 * g + 8]
+            lows.append(frame[24:28])
+        x_ref[384 + 8 * i : 392 + 8 * i, :] = jnp.concatenate(lows, axis=0)
     xn = modulate(x_ref[...], mod_ref[3:4, :], mod_ref[4:5, :])
-    for copy in copies[:3]:
-        copy.wait()
     packed = jnp.dot(xn, w_ref[...], preferred_element_type=F32)
-    q_ref[...] = (packed[:, :WIDTH] * QSCALE).astype(BF16)
+    q_ref[:, ROWS:] = jnp.zeros((WIDTH, PADDED - ROWS), BF16)
+    q_ref[:, :ROWS] = (packed[:, :WIDTH] * QSCALE).T.astype(BF16)
     k_ref[...] = packed[:, WIDTH : 2 * WIDTH].astype(BF16)
     vt_ref[...] = packed[:, 2 * WIDTH :].T
-    lane = lax.broadcasted_iota(jnp.int32, (1, 256), 1)
-    same = lax.broadcasted_iota(jnp.int32, (128, 256), 0) % 8 == lax.broadcasted_iota(jnp.int32, (128, 256), 1) % 8
-    tail = jnp.where(lax.broadcasted_iota(jnp.int32, (AUG - HEAD_DIM, 128), 0) == 0, 1.0, 0.0)
-
-    for g in range(4):
-        rows = slice(g * 128, (g + 1) * 128)
-        for p in range(8):
-            inside = 16 * p
-            window = slice(128 * p, 128 * p + 256)
-            q = q_ref[rows, window]
-            none = jnp.zeros((), BF16)
-            first = jnp.where((lane >= inside) & (lane < inside + HEAD_DIM), q, none)
-            second = jnp.where((lane >= inside + HEAD_DIM) & (lane < inside + 2 * HEAD_DIM), q, none)
-            queries = jnp.concatenate([first, second], axis=0)
-            scores = lax.dot_general(k_ref[rows, window], queries, NT, preferred_element_type=F32)
-            scores = jnp.where(same, scores, -1e30)
-            top = jnp.max(scores, axis=0, keepdims=True)
-            weights = jnp.exp2(scores - top).astype(BF16)
-            at = 2 * HEAD_DIM * p
-            values = jnp.concatenate(
-                [vt_ref[at : at + HEAD_DIM, rows], tail, vt_ref[at + HEAD_DIM : at + 2 * HEAD_DIM, rows], tail], axis=0
-            ).astype(BF16)
-            total = jnp.dot(values, weights, preferred_element_type=F32)
-            a = total[:HEAD_DIM, :128] / total[HEAD_DIM : HEAD_DIM + 1, :128]
-            b = total[AUG : AUG + HEAD_DIM, 128:] / total[AUG + HEAD_DIM : AUG + HEAD_DIM + 1, 128:]
-            att_ref[at : at + 2 * HEAD_DIM, rows] = jnp.concatenate([a, b], axis=0).astype(BF16)
-    copies[3].wait()
-    projected = lax.dot_general(att_ref[...], wo_ref[...], TN, preferred_element_type=F32)
+
+    row = lax.broadcasted_iota(jnp.int32, (256, 1), 0)
+    none = jnp.zeros((), BF16)
+
+    def rows_of(g):
+        return slice(g * 128, min(g * 128 + 128, ROWS))
+
+    def score(g, p):
+        queries = q_ref[128 * p : 128 * p + 256, g * 128 : g * 128 + 128]
+        inside = 16 * p
+        first = jnp.where((row >= inside) & (row < inside + HEAD_DIM), queries, none)
+        second = jnp.where((row >= inside + HEAD_DIM) & (row < inside + 2 * HEAD_DIM), queries, none)
+        keys = k_ref[rows_of(g), 128 * p : 128 * p + 256]
+        return jnp.dot(keys, jnp.concatenate([first, second], axis=1), preferred_element_type=F32)
+
+    def weigh(g, scores):
+        every = 8 if g < 3 else 4
+        shape = scores.shape
+        key_token = lax.broadcasted_iota(jnp.int32, shape, 0) % every
+        same = key_token == lax.broadcasted_iota(jnp.int32, shape, 1) % every
+        scores = jnp.where(same, scores, -1e30)
+        top = jnp.max(scores, axis=0, keepdims=True)
+        return jnp.exp2(scores - top).astype(BF16)
+
+    def value(g, p, weights):
+        at = 2 * HEAD_DIM * p
+        tail = jnp.where(lax.broadcasted_iota(jnp.int32, (AUG - HEAD_DIM, weights.shape[0]), 0) == 0, 1.0, 0.0)
+        first = vt_ref[at : at + HEAD_DIM, rows_of(g)]
+        second = vt_ref[at + HEAD_DIM : at + 2 * HEAD_DIM, rows_of(g)]
+        values = jnp.concatenate([first, tail, second, tail], axis=0).astype(BF16)
+        return jnp.dot(values, weights, preferred_element_type=F32)
+
+    def finish(g, p, total):
+        at = 2 * HEAD_DIM * p
+        first = total[:HEAD_DIM, :128] / total[HEAD_DIM : HEAD_DIM + 1, :128]
+        second = total[AUG : AUG + HEAD_DIM, 128:] / total[AUG + HEAD_DIM : AUG + HEAD_DIM + 1, 128:]
+        both = jnp.concatenate([first, second], axis=0).astype(BF16)
+        att_ref[at : at + 2 * HEAD_DIM, g * 128 : g * 128 + 128] = both
+
+    order = [(g, p) for g in range(4) for p in range(8)]
+    apart = 4
+    scores, totals = {}, {}
+    for i in range(len(order) + 2 * apart):
+        if i < len(order):
+            scores[i] = score(*order[i])
+        j = i - apart
+        if 0 <= j < len(order):
+            g, p = order[j]
+            totals[j] = value(g, p, weigh(g, scores.pop(j)))
+        k = i - 2 * apart
+        if 0 <= k < len(order):
+            finish(*order[k], totals.pop(k))
+
+    projected = lax.dot_general(att_ref[:, :ROWS], wo_ref[...], TN, preferred_element_type=F32)
     x_ref[...] = x_ref[...] + mod_ref[5:6, :] * projected
     for f in range(16):
-        pieces = [x_ref[(g * 16 + f) * 8 : (g * 16 + f + 1) * 8, :] for g in range(4)]
-        out_ref[f] = jnp.concatenate(pieces, axis=0).astype(BF16)
+        pieces = [x_ref[(g * 16 + f) * 8 : (g * 16 + f + 1) * 8, :] for g in range(3)]
+        last = x_ref[384 + 8 * (f // 2) : 392 + 8 * (f // 2), :]
+        if f % 2:
+            last = jnp.concatenate([last[4:], last[:4]], axis=0)
+        out_ref[f] = jnp.concatenate(pieces + [last], axis=0).astype(BF16)
 
 
 def temporal(mid, mod, w, wo):
     return pl.pallas_call(
         temporal_kernel,
-        in_specs=[VMEM, VMEM, HBM, HBM],
+        in_specs=[VMEM] * 4,
         out_specs=VMEM,
         out_shape=jax.ShapeDtypeStruct((16, 32, WIDTH), BF16),
         scratch_shapes=[
-            pltpu.VMEM((512, WIDTH), F32),
-            pltpu.VMEM((WIDTH, 3 * WIDTH), BF16),
-            pltpu.VMEM((WIDTH, WIDTH), BF16),
-            pltpu.VMEM((512, WIDTH), BF16),
-            pltpu.VMEM((512, WIDTH), BF16),
-            pltpu.VMEM((WIDTH, 512), F32),
-            pltpu.VMEM((WIDTH, 512), BF16),
-            pltpu.SemaphoreType.DMA((4,)),
+            pltpu.VMEM((ROWS, WIDTH), F32),
+            pltpu.VMEM((WIDTH, PADDED), BF16),
+            pltpu.VMEM((ROWS, WIDTH), BF16),
+            pltpu.VMEM((WIDTH, ROWS), F32),
+            pltpu.VMEM((WIDTH, PADDED), BF16),
         ],
-        compiler_params=params(),
+        compiler_params=params(24),
         cost_estimate=pl.CostEstimate(flops=6_000_000_000, bytes_accessed=14_000_000, transcendentals=1_000_000),
         name="temporal_block",
     )(mid, mod, w, wo)

time: 119 us -> 107 us (0.90)
  Pallas kernels: 57.3 us -> 42.1 us
  local copies, waits for them, and re-layouts: 3.1 us -> 7.98 us
  waiting for transfers between devices: 5.97 us -> 3.97 us
    pallas_call x1, Pallas kernels: 18.6 us -> 8.26 us  [temporal(): pl.pallas_call(temporal_kernel, in_specs=[VMEM] * 4, out_specs=VMEM, out_...]
    unnamed x14 -> x22, local copies, waits for them, and re-layouts: 2.04 us -> 6.92 us
    pallas_call x1, Pallas kernels: 15.6 us -> 12.9 us  [far(): pl.pallas_call(far_kernel, in_specs=[SMEM, VMEM, VMEM, HBM] + [VMEM] * 5,...]
    ppermute x1, waiting for transfers between devices: 4.34 us -> 2.33 us  [local(): there = lax.ppermute(own, 'head', swap_chip)]
    pallas_call x1, Pallas kernels: 17.5 us -> 16.2 us  [near(): pl.pallas_call(near_kernel, in_specs=[SMEM, VMEM, VMEM, VMEM, HBM], out_s...]
where the time goes in v3:
time: 107 us; the launch traced here: 106 us
  blocking collectives  48.3 us (45%)
  Pallas kernels  42.1 us (39%)
  local copies, waits for them, and re-layouts  7.98 us (7%)
  waiting for transfers between devices  3.97 us (4%)
  starting transfers between devices  3.71 us (3%)
    all_to_all x1, blocking collectives, local(): lax.all_to_all(middle, 'tm', split_axis=0, concat_axis=0, tiled=True)  27.1 us
    all_to_all x1, blocking collectives, local(): back = lax.all_to_all(done, 'tm', split_axis=0, concat_axis=0, tiled=True)  21.2 us
    pallas_call x1, Pallas kernels, near(): pl.pallas_call(near_kernel, in_specs=[SMEM, VMEM, VMEM, VMEM, HBM], out_s...  16.2 us
    pallas_call x1, Pallas kernels, far(): pl.pallas_call(far_kernel, in_specs=[SMEM, VMEM, VMEM, HBM] + [VMEM] * 5,...  12.9 us
    pallas_call x1, Pallas kernels, temporal(): pl.pallas_call(temporal_kernel, in_specs=[VMEM] * 4, out_specs=VMEM, out_...  8.26 us
    unnamed x22, local copies, waits for them, and re-layouts  6.92 us
    ppermute x1, starting transfers between devices, local(): there = lax.ppermute(own, 'head', swap_chip)  3.11 us
    pallas_call x1, Pallas kernels, project(): pl.pallas_call(project_kernel, in_specs=[SMEM, VMEM, VMEM, HBM], out_spec...  2.9 us
  transfers between devices with their start and end apart: 4, of which 2 were waited for; matrix products, arithmetic and copies ran while one was open for 0% of the time, Pallas kernels for 18%

profile of v3, /device:TPU:0, one launch (start us, length us, event | category | flops | bytes accessed | tf_op | source)
XLA Modules:
  0.0 106.1 jit_solution(13182840201863518846)
XLA Ops:
  0.0 0.0 collective-permute-start.1
  0.0 3.1 %collective-permute-start = (bf16[448,1152]{1,0:T(8,128)(2,1)}, bf16[448,1152]{1,0:T(8,128)(2,1)S(1)}, u32[]{:S(2)}, u32[]{:S(2)}) collective-permute-start(bf16[448,1152]{1,0:T(8,128)(2,1)} %bitcast.4), channel_id=1, source_target_pairs={{0,2},{1,3},{2,0},{3,1},{4,6},{5,7},{6,4},{7,5},{8,10},{9,11},{10,... | collective-permute-start | bytes 3096584 | tf_op jit(solution)/shard_map/ppermute | solution.py:347
  3.1 0.0 collective-permute-done.1.xp_ref
  3.1 0.0 copy-start
  3.1 3.3 %copy-done = bf16[1152,3456]{1,0:T(8,128)(2,1)S(1)} copy-done((bf16[1152,3456]{1,0:T(8,128)(2,1)S(1)}, bf16[1152,3456]{1,0:T(8,128)(2,1)}, u32[]{:S(2)}) %copy-start) | copy-done | bytes 7962648
  6.4 0.0 copy-start.2
  6.4 1.2 %copy-done.2 = bf16[1,448,1152]{2,1,0:T(8,128)(2,1)S(1)} copy-done((bf16[1,448,1152]{2,1,0:T(8,128)(2,1)S(1)}, bf16[1,448,1152]{2,1,0:T(8,128)(2,1)}, u32[]{:S(2)}) %copy-start.2) | copy-done | bytes 1032216
  7.6 0.0 copy-start.4
  7.6 0.8 copy-done.4
  8.4 16.2 %near_tokens.1 = (bf16[896,640]{1,0:T(8,128)(2,1)S(1)}, f32[8,80,896]{2,1,0:T(8,128)S(1)}, f32[8,8,896]{2,1,0:T(8,128)S(1)}) custom-call(s32[1]{0:T(128)} %bitcast.core_ref, bf16[448,1152]{1,0:T(8,128)(2,1)S(1)} %bitcast.5, bf16[448,1152]{1,0:T(8,128)(2,1)S(1)} %collective-permute-done.1.xp_ref, f32[6,1152]{1,0:T(8,128)S(1)} %copy-done.4, ...), custom_call_target="tpu_custom_call" | custom-call | flops 20000000000 | bytes 10000000 | tf_op jit(solution)/shard_map/near_tokens/pallas_call | solution.py:129
  24.6 0.0 copy-start.7
  24.6 2.3 %collective-permute-done.x_ref = bf16[448,1152]{1,0:T(8,128)(2,1)S(1)} collective-permute-done((bf16[448,1152]{1,0:T(8,128)(2,1)}, bf16[448,1152]{1,0:T(8,128)(2,1)S(1)}, u32[]{:S(2)}, u32[]{:S(2)}) %collective-permute-start) | collective-permute-done | bytes 1032224 | tf_op jit(solution)/shard_map/ppermute | solution.py:347
  26.9 0.0 collective-permute-start.2
  26.9 0.0 slice-start
  26.9 2.9 %far_keys.1 = (bf16[448,640]{1,0:T(8,128)(2,1)S(1)}, f32[640,448]{1,0:T(8,128)S(1)}) custom-call(s32[1]{0:T(128)} %bitcast.core_ref, bf16[448,1152]{1,0:T(8,128)(2,1)S(1)} %collective-permute-done.x_ref, f32[6,1152]{1,0:T(8,128)S(1)} %copy-done.4, bf16[1152,3456]{1,0:T(8,128)(2,1)S(1)} %copy-done), custom_call_target="tpu_custom_call" | custom-call | flops 2000000000 | bytes 6000000 | tf_op jit(solution)/shard_map/far_keys/pallas_call | solution.py:164
  29.8 0.0 copy-done.7
  29.9 0.0 collective-permute-done.2.x_ref
  29.9 0.0 copy-start.8
  29.9 1.6 %copy-done.8 = f32[8,80,896]{2,1,0:T(8,128)S(1)} copy-done((f32[8,80,896]{2,1,0:T(8,128)S(1)}, f32[8,80,896]{2,1,0:T(8,128)}, u32[]{:S(2)}) %copy-start.8) | copy-done | bytes 2293784
  31.5 0.0 copy-start.1
  31.5 0.0 copy-start.3
  31.5 0.0 slice-start.1
  31.5 12.9 %far_tokens.1 = (bf16[576,448]{1,0:T(8,128)(2,1)S(1)}, bf16[576,512]{1,0:T(8,128)(2,1)S(1)}) custom-call(s32[1]{0:T(128)} %bitcast.core_ref, bf16[448,1152]{1,0:T(8,128)(2,1)S(1)} %collective-permute-done.2.x_ref, f32[6,1152]{1,0:T(8,128)S(1)} %copy-done.4, bf16[1152,3456]{1,0:T(8,128)(2,1)S(1)} %copy-done, bf16[448,640]{1,0:T(8,128)(2,1)S(1)} %get-tuple-element.16.k1_ref, ...), custom_call_target="tpu_custom_call" | custom-call | flops 17999998976 | bytes 10000000 | tf_op jit(solution)/shard_map/far_tokens/pallas_call | solution.py:203
  44.4 0.6 collective-permute-start.3
  45.0 1.6 %collective-permute-done.3.other_ref = bf16[576,512]{1,0:T(8,128)(2,1)S(1)} collective-permute-done((bf16[576,512]{1,0:T(8,128)(2,1)S(1)}, bf16[576,512]{1,0:T(8,128)(2,1)S(1)}, u32[]{:S(2)}, u32[]{:S(2)}) %collective-permute-start.3) | collective-permute-done | bytes 589856 | tf_op jit(solution)/shard_map/ppermute | solution.py:353
  46.6 0.0 copy-done.1
  46.6 0.0 copy-done.3
  46.6 0.0 copy-start.6
  46.7 1.8 %spatial_out.1 = bf16[16,32,1152]{2,1,0:T(8,128)(2,1)S(1)} custom-call(s32[1]{0:T(128)} %bitcast.core_ref, bf16[576,448]{1,0:T(8,128)(2,1)S(1)} %get-tuple-element.21.mine_ref, bf16[576,512]{1,0:T(8,128)(2,1)S(1)} %collective-permute-done.3.other_ref, bf16[448,1152]{1,0:T(8,128)(2,1)S(1)} %bitcast.6, f32[6,1152]{1,0:T(8,128)S(1)} %copy-done.4, ...), custom_call_target="tpu_custom_call" | custom-call | flops 1200000000 | bytes 6000000 | tf_op jit(solution)/shard_map/spatial_out/pallas_call | solution.py:232
  48.5 0.0 copy-start.5
  48.5 27.1 %all_to_all.10.mid_ref = bf16[16,32,1152]{2,1,0:T(8,128)(2,1)S(1)} all-to-all(bf16[16,32,1152]{2,1,0:T(8,128)(2,1)S(1)} %spatial_out.1), channel_id=1, replica_groups=mesh['dp'=2,'tm'=16,'head'=4] {'tm'}, dimensions={0} | all-to-all | bytes 2359296 | tf_op jit(solution)/shard_map/all_to_all | solution.py:355
  75.6 0.0 slice-done
  75.6 0.0 slice-done.1
  75.6 0.0 copy-done.6
  75.6 0.0 copy-done.5
  75.6 8.3 %temporal_block.1 = bf16[16,32,1152]{2,1,0:T(8,128)(2,1)S(1)} custom-call(bf16[16,32,1152]{2,1,0:T(8,128)(2,1)S(1)} %all_to_all.10.mid_ref, f32[6,1152]{1,0:T(8,128)S(1)} %copy-done.5, bf16[1152,3456]{1,0:T(8,128)(2,1)S(1)} %bitcast.8, bf16[1152,1152]{1,0:T(8,128)(2,1)S(1)} %copy-done.6), custom_call_target="tpu_custom_call" | custom-call | flops 6000000000 | bytes 14000000 | tf_op jit(solution)/shard_map/temporal_block/pallas_call | solution.py:323
  83.8 21.2 %all_to_all.11 = bf16[16,32,1152]{2,1,0:T(8,128)(2,1)S(1)} all-to-all(bf16[16,32,1152]{2,1,0:T(8,128)(2,1)S(1)} %temporal_block.1), channel_id=1, replica_groups=mesh['dp'=2,'tm'=16,'head'=4] {'tm'}, dimensions={0} | all-to-all | bytes 2359296 | tf_op jit(solution)/shard_map/all_to_all | solution.py:357
  105.1 1.1 reshape.7
  (1 shorter events, 0.0 us)
Async XLA Ops:
  0.0 3.1 %collective-permute-start.1 = (bf16[448,1152]{1,0:T(8,128)(2,1)}, bf16[448,1152]{1,0:T(8,128)(2,1)S(1)}, u32[]{:S(2)}, u32[]{:S(2)}) collective-permute-start(bf16[448,1152]{1,0:T(8,128)(2,1)} %bitcast.3), channel_id=1, source_target_pairs={{0,1},{1,0},{2,3},{3,2},{4,5},{5,4},{6,7},{7,6},{8,9},{9,8},{10,11... | collective-permute-start | bytes 3096584 | tf_op jit(solution)/shard_map/ppermute | solution.py:346
  0.0 26.9 %collective-permute-start = (bf16[448,1152]{1,0:T(8,128)(2,1)}, bf16[448,1152]{1,0:T(8,128)(2,1)S(1)}, u32[]{:S(2)}, u32[]{:S(2)}) collective-permute-start(bf16[448,1152]{1,0:T(8,128)(2,1)} %bitcast.4), channel_id=1, source_target_pairs={{0,2},{1,3},{2,0},{3,1},{4,6},{5,7},{6,4},{7,5},{8,10},{9,11},{10,... | collective-permute-start | bytes 3096584 | tf_op jit(solution)/shard_map/ppermute | solution.py:347
  3.1 3.3 %copy-start = (bf16[1152,3456]{1,0:T(8,128)(2,1)S(1)}, bf16[1152,3456]{1,0:T(8,128)(2,1)}, u32[]{:S(2)}) copy-start(bf16[1152,3456]{1,0:T(8,128)(2,1)} %w_hbm.5) | copy-start | bytes 23887876
  6.4 1.2 %copy-start.2 = (bf16[1,448,1152]{2,1,0:T(8,128)(2,1)S(1)}, bf16[1,448,1152]{2,1,0:T(8,128)(2,1)}, u32[]{:S(2)}) copy-start(bf16[1,448,1152]{2,1,0:T(8,128)(2,1)} %param.6) | copy-start | bytes 3096580
  7.6 0.8 copy-start.4
  24.6 5.3 %copy-start.7 = (f32[8,80,896]{2,1,0:T(8,128)}, f32[8,80,896]{2,1,0:T(8,128)S(1)}, u32[]{:S(2)}) copy-start(f32[8,80,896]{2,1,0:T(8,128)S(1)} %get-tuple-element.19.acc_ref) | copy-start | bytes 6881284
  26.9 2.9 %collective-permute-start.2 = (bf16[448,1152]{1,0:T(8,128)(2,1)S(1)}, bf16[448,1152]{1,0:T(8,128)(2,1)S(1)}, u32[]{:S(2)}, u32[]{:S(2)}) collective-permute-start(bf16[448,1152]{1,0:T(8,128)(2,1)S(1)} %collective-permute-done.x_ref), channel_id=1, source_target_pairs={{0,1},{1,0},{2,3},{3,2},{4,5},{5,4},{6,7},{7,6},{8,9},{9,8},{10,11... | collective-permute-start | bytes 3096584 | tf_op jit(solution)/shard_map/ppermute | solution.py:351
  26.9 48.6 %slice-start = ((s8[7962624]{0:T(1024)(128)(4,1)}), s8[4194304]{0:T(1024)(128)(4,1)S(1)}, s32[]{:S(2)}) async-start(s8[7962624]{0:T(1024)(128)(4,1)} %bitcast.7), calls=%async_computation.2 | async-start | bytes 8388608
  29.9 1.6 %copy-start.8 = (f32[8,80,896]{2,1,0:T(8,128)S(1)}, f32[8,80,896]{2,1,0:T(8,128)}, u32[]{:S(2)}) copy-start(f32[8,80,896]{2,1,0:T(8,128)} %copy-done.7) | copy-start | bytes 6881284
  31.5 15.1 %copy-start.1 = (bf16[1152,1152]{1,0:T(8,128)(2,1)S(1)}, bf16[1152,1152]{1,0:T(8,128)(2,1)}, u32[]{:S(2)}) copy-start(bf16[1152,1152]{1,0:T(8,128)(2,1)} %wo_ref.2) | copy-start | bytes 7962628
  31.5 15.1 %copy-start.3 = (bf16[1,448,1152]{2,1,0:T(8,128)(2,1)S(1)}, bf16[1,448,1152]{2,1,0:T(8,128)(2,1)}, u32[]{:S(2)}) copy-start(bf16[1,448,1152]{2,1,0:T(8,128)(2,1)} %param.6) | copy-start | bytes 3096580
  31.5 44.0 %slice-start.1 = ((s8[7962624]{0:T(1024)(128)(4,1)}), s8[3768320]{0:T(1024)(128)(4,1)S(1)}, s32[]{:S(2)}) async-start(s8[7962624]{0:T(1024)(128)(4,1)} %bitcast.7), calls=%async_computation.3 | async-start | bytes 7536640
  44.4 2.2 %collective-permute-start.3 = (bf16[576,512]{1,0:T(8,128)(2,1)S(1)}, bf16[576,512]{1,0:T(8,128)(2,1)S(1)}, u32[]{:S(2)}, u32[]{:S(2)}) collective-permute-start(bf16[576,512]{1,0:T(8,128)(2,1)S(1)} %get-tuple-element.22), channel_id=1, source_target_pairs={{0,1},{1,0},{2,3},{3,2},{4,5},{5,4},{6,7},{7,6},{8,9},{9,8},{10,11... | collective-permute-start | bytes 1769480 | tf_op jit(solution)/shard_map/ppermute | solution.py:353
  46.6 28.9 %copy-start.6 = (bf16[1152,1152]{1,0:T(8,128)(2,1)S(1)}, bf16[1152,1152]{1,0:T(8,128)(2,1)}, u32[]{:S(2)}) copy-start(bf16[1152,1152]{1,0:T(8,128)(2,1)} %wo_ref.3) | copy-start | bytes 7962628
  48.5 27.1 %copy-start.5 = (f32[6,1152]{1,0:T(8,128)S(1)}, f32[6,1152]{1,0:T(8,128)}, u32[]{:S(2)}) copy-start(f32[6,1152]{1,0:T(8,128)} %mod_ref.9) | copy-start | bytes 82948

commit v4 on v3

v4 whole, which is shorter than its diff:
```python
import math

import jax
import jax.numpy as jnp
from jax import lax
from jax.experimental import pallas as pl
from jax.experimental.pallas import tpu as pltpu
from jax.sharding import PartitionSpec as P

HEADS = 16
HEAD_DIM = 72
WIDTH = 1152
ROWS = 448
LANES = 896
WINDOW = 640
HALF_COLS = 576
AUG = 80
PADDED = 512
TILE = 512
QSCALE = math.log2(math.e) / math.sqrt(HEAD_DIM)
NT = (((1,), (1,)), ((), ()))
TN = (((0,), (0,)), ((), ()))
BF16 = jnp.bfloat16
F32 = jnp.float32
VMEM = pl.BlockSpec(memory_space=pltpu.VMEM)
SMEM = pl.BlockSpec(memory_space=pltpu.SMEM)
HBM = pl.BlockSpec(memory_space=pltpu.HBM)
EXCESS = 64.0


def params(mebibytes):
    return pltpu.CompilerParams(vmem_limit_bytes=mebibytes * 1024 * 1024)


def modulate(values, shift_vec, scale_vec):
    values = values.astype(F32)
    average = jnp.mean(values, axis=-1, keepdims=True)
    centred = values - average
    variance = jnp.mean(centred * centred, axis=-1, keepdims=True)
    normed = centred * lax.rsqrt(variance + 1e-06)
    return (normed * (1.0 + scale_vec) + shift_vec).astype(BF16)


def window_copy(w_hbm, third, core, place, sem):
    start = pl.multiple_of(third * WIDTH + core * 512, 128)
    return pltpu.make_async_copy(w_hbm.at[:, pl.ds(start, WINDOW)], place, sem)


def head_window(head, core):
    offset = head * HEAD_DIM + core * 64
    start = pl.multiple_of(jnp.minimum(offset // 128, 3) * 128, 128)
    return offset, start, offset - start


def head_operands(head, core, q_ref, blocks):
    offset, start, inside = head_window(head, core)
    lane = lax.broadcasted_iota(jnp.int32, (1, 256), 1)
    mine = (lane >= inside) & (lane < inside + HEAD_DIM)
    queries = jnp.where(mine, q_ref[:, pl.ds(start, 256)], jnp.zeros((), BF16))
    keys, values = [], []
    for k_ref, vt_ref in blocks:
        keys.append(k_ref[:, pl.ds(start, 256)])
        first = lax.broadcasted_iota(jnp.int32, (AUG - HEAD_DIM, k_ref.shape[0]), 0) == 0
        vt = vt_ref[pl.ds(pl.multiple_of(offset, 8), HEAD_DIM), :]
        values.append(jnp.concatenate([vt, jnp.where(first, 1.0, 0.0)], axis=0).astype(BF16))
    return queries, keys, values


def attend_head(head, core, q_ref, blocks, old, known_top):
    queries, keys, values = head_operands(head, core, q_ref, blocks)
    starts = list(range(0, LANES, TILE))

    def score(s):
        part = queries[s : min(s + TILE, LANES)]
        return [lax.dot_general(k, part, NT, preferred_element_type=F32) for k in keys]

    out = []
    ahead = score(starts[0])
    for i, s in enumerate(starts):
        scores = ahead
        if i + 1 < len(starts):
            ahead = score(starts[i + 1])
        lanes = slice(s, s + scores[0].shape[1])
        tops = [jnp.max(part, axis=0, keepdims=True) for part in scores]
        top = tops[0]
        for more in tops[1:]:
            top = jnp.maximum(top, more)
        total = None
        reference = top
        if old is not None:
            acc_ref, top_ref = old
            before = top_ref[head, 0:1, lanes]
            total = acc_ref[head, :, lanes]
            if known_top:
                reference = before
            else:
                reference = jnp.maximum(top, before)
                total = total * jnp.exp2(before - reference)
        for value, part in zip(values, scores):
            term = jnp.dot(value, jnp.exp2(part - reference).astype(BF16), preferred_element_type=F32)
            total = term if total is None else total + term
        out.append((s, total, reference, top))
    return out


def keys_values(xn, w_ref, k_ref, vt_ref):
    packed = jnp.dot(xn, w_ref[...], preferred_element_type=F32)
    k_ref[...] = packed[:, :WINDOW].astype(BF16)
    vt_ref[...] = packed[:, WINDOW:].T


def near_kernel(
    core_ref, xo_hbm, xp_ref, mod_hbm, w_hbm, q_ref, acc_ref, top_ref, mod_ref, w_ref, wq_ref, xo_ref, xn_ref, k_ref, vt_ref, sems
):
    core = core_ref[0]
    own = pltpu.make_async_copy(xo_hbm, xo_ref, sems.at[3])
    mod = pltpu.make_async_copy(mod_hbm, mod_ref, sems.at[4])
    mod.start()
    own.start()
    copies = [
        window_copy(w_hbm, 0, core, wq_ref, sems.at[0]),
        window_copy(w_hbm, 1, core, w_ref.at[:, :WINDOW], sems.at[1]),
        window_copy(w_hbm, 2, core, w_ref.at[:, WINDOW:], sems.at[2]),
    ]
    for copy in copies:
        copy.start()
    mod.wait()
    xn_ref[ROWS:, :] = modulate(xp_ref[...], mod_ref[0:1, :], mod_ref[1:2, :])
    own.wait()
    xn_ref[0:ROWS, :] = modulate(xo_ref[...], mod_ref[0:1, :], mod_ref[1:2, :])
    copies[0].wait()
    queries = jnp.dot(xn_ref[...], wq_ref[...], preferred_element_type=F32)
    q_ref[...] = (queries * QSCALE).astype(BF16)
    copies[1].wait()
    copies[2].wait()
    keys_values(xn_ref[...], w_ref, k_ref, vt_ref)

    def pair(p, carry):
        for h in range(2):
            head = 2 * p + h
            for s, total, top, _ in attend_head(head, core, q_ref, ((k_ref, vt_ref),), None, False):
                width = total.shape[1]
                acc_ref[head, :, s : s + width] = total
                top_ref[head, :, s : s + width] = jnp.broadcast_to(top, (8, width))
        return carry

    lax.fori_loop(0, 4, pair, 0)


def near(core, xo, xp, mod, w):
    return pl.pallas_call(
        near_kernel,
        in_specs=[SMEM, HBM, VMEM, HBM, HBM],
        out_specs=[VMEM] * 5,
        out_shape=[
            jax.ShapeDtypeStruct((LANES, WINDOW), BF16),
            jax.ShapeDtypeStruct((8, AUG, LANES), F32),
            jax.ShapeDtypeStruct((8, 8, LANES), F32),
            jax.ShapeDtypeStruct((6, WIDTH), F32),
            jax.ShapeDtypeStruct((WIDTH, 2 * WINDOW), BF16),
        ],
        scratch_shapes=[
            pltpu.VMEM((WIDTH, WINDOW), BF16),
            pltpu.VMEM((ROWS, WIDTH), BF16),
            pltpu.VMEM((LANES, WIDTH), BF16),
            pltpu.VMEM((LANES, WINDOW), BF16),
            pltpu.VMEM((WINDOW, LANES), F32),
            pltpu.SemaphoreType.DMA((5,)),
        ],
        compiler_params=params(40),
        cost_estimate=pl.CostEstimate(flops=1_000_000, bytes_accessed=100_000, transcendentals=0),
        name="near_tokens",
    )(core, xo, xp, mod, w)


def project_kernel(x_ref, mod_ref, w_ref, k_ref, vt_ref):
    xn = modulate(x_ref[...], mod_ref[0:1, :], mod_ref[1:2, :])
    keys_values(xn, w_ref, k_ref, vt_ref)


def project(x, mod, w):
    return pl.pallas_call(
        project_kernel,
        in_specs=[VMEM] * 3,
        out_specs=[VMEM] * 2,
        out_shape=[jax.ShapeDtypeStruct((ROWS, WINDOW), BF16), jax.ShapeDtypeStruct((WINDOW, ROWS), F32)],
        compiler_params=params(14),
        cost_estimate=pl.CostEstimate(flops=1_000_000, bytes_accessed=100_000, transcendentals=0),
        name="far_keys",
    )(x, mod, w)


def far_kernel(
    core_ref, x_ref, mod_ref, w_ref, k1_ref, vt1_ref, q_ref, acc_ref, top_ref, next_hbm, own_ref, peer_ref, next_ref, k_ref, vt_ref, over_ref, sem
):
    core = core_ref[0]
    ahead = pltpu.make_async_copy(next_hbm, next_ref, sem)
    ahead.start()
    xn = modulate(x_ref[...], mod_ref[0:1, :], mod_ref[1:2, :])
    keys_values(xn, w_ref, k_ref, vt_ref)
    blocks = ((k1_ref, vt1_ref), (k_ref, vt_ref))
    over_ref[...] = jnp.zeros_like(over_ref)

    def attend(known_top):
        def pair(p, carry):
            halves = []
            for h in range(2):
                parts = attend_head(2 * p + h, core, q_ref, blocks, (acc_ref, top_ref), known_top)
                if known_top:
                    for s, total, reference, top in parts:
                        lanes = slice(s, s + total.shape[1])
                        over_ref[0:1, lanes] = jnp.maximum(over_ref[0:1, lanes], top - reference)
                halves.append(
                    jnp.concatenate([t[:HEAD_DIM] / t[HEAD_DIM : HEAD_DIM + 1] for _, t, _, _ in parts], axis=1)
                )
            both = jnp.concatenate(halves, axis=0)
            rows = pl.ds(pl.multiple_of(p * 2 * HEAD_DIM, 16), 2 * HEAD_DIM)
            own_ref[rows, :] = both[:, :ROWS].astype(BF16)
            peer_ref[rows, :] = jnp.concatenate(
                [both[:, ROWS:], jnp.zeros((2 * HEAD_DIM, PADDED - ROWS), F32)], axis=1
            ).astype(BF16)
            return carry

        lax.fori_loop(0, 4, pair, 0)

    attend(True)

    @pl.when(jnp.max(over_ref[...]) > EXCESS)
    def _():
        attend(False)

    ahead.wait()


def far(core, x, mod, w, k1, vt1, q, acc, top, following):
    return pl.pallas_call(
        far_kernel,
        in_specs=[SMEM] + [VMEM] * 8 + [HBM],
        out_specs=[VMEM] * 3,
        out_shape=[
            jax.ShapeDtypeStruct((HALF_COLS, ROWS), BF16),
            jax.ShapeDtypeStruct((HALF_COLS, PADDED), BF16),
            jax.ShapeDtypeStruct((WIDTH, 3 * WIDTH), BF16),
        ],
        scratch_shapes=[
            pltpu.VMEM((ROWS, WINDOW), BF16),
            pltpu.VMEM((WINDOW, ROWS), F32),
            pltpu.VMEM((8, LANES), F32),
            pltpu.SemaphoreType.DMA,
        ],
        compiler_params=params(32),
        cost_estimate=pl.CostEstimate(flops=18_000_000_000, bytes_accessed=10_000_000, transcendentals=6_400_000),
        name="far_tokens",
    )(core, x, mod, w, k1, vt1, q, acc, top, following)


def join_kernel(core_ref, mine_ref, other_ref, x_ref, mod_ref, wo_ref, out_ref, att_ref):
    core = core_ref[0]
    att_ref[pl.ds(pl.multiple_of(core * HALF_COLS, 16), HALF_COLS), :] = mine_ref[...]
    att_ref[pl.ds(pl.multiple_of((1 - core) * HALF_COLS, 16), HALF_COLS), :] = other_ref[:, :ROWS]
    projected = lax.dot_general(att_ref[...], wo_ref[...], TN, preferred_element_type=F32)
    middle = x_ref[...].astype(F32) + mod_ref[2:3, :] * projected
    for d in range(16):
        for i in range(7):
            out_ref[d, i] = middle[28 * d + 4 * i : 28 * d + 4 * i + 4].astype(BF16)


def join(core, mine, other, x, mod, wo):
    return pl.pallas_call(
        join_kernel,
        in_specs=[SMEM] + [VMEM] * 5,
        out_specs=VMEM,
        out_shape=jax.ShapeDtypeStruct((16, 7, 4, WIDTH), BF16),
        scratch_shapes=[pltpu.VMEM((WIDTH, ROWS), BF16)],
        compiler_params=params(14),
        cost_estimate=pl.CostEstimate(flops=1_200_000_000, bytes_accessed=6_000_000, transcendentals=0),
        name="spatial_out",
    )(core, mine, other, x, mod, wo)


def temporal_kernel(mid_ref, mod_ref, w_ref, wo_ref, out_ref, x_ref, q_ref, k_ref, vt_ref, att_ref):
    for f in range(16):
        for i in range(7):
            at = ((i // 2 * 16) + f) * 8 + i % 2 * 4 if i < 6 else 384 + 4 * f
            x_ref[at : at + 4, :] = mid_ref[f, i].astype(F32)
    xn = modulate(x_ref[...], mod_ref[3:4, :], mod_ref[4:5, :])
    packed = jnp.dot(xn, w_ref[...], preferred_element_type=F32)
    q_ref[:, ROWS:] = jnp.zeros((WIDTH, PADDED - ROWS), BF16)
    q_ref[:, :ROWS] = (packed[:, :WIDTH] * QSCALE).T.astype(BF16)
    k_ref[...] = packed[:, WIDTH : 2 * WIDTH].astype(BF16)
    vt_ref[...] = packed[:, 2 * WIDTH :].T

    row = lax.broadcasted_iota(jnp.int32, (256, 1), 0)
    none = jnp.zeros((), BF16)

    def rows_of(g):
        return slice(g * 128, min(g * 128 + 128, ROWS))

    def score(g, p):
        queries = q_ref[128 * p : 128 * p + 256, g * 128 : g * 128 + 128]
        inside = 16 * p
        first = jnp.where((row >= inside) & (row < inside + HEAD_DIM), queries, none)
        second = jnp.where((row >= inside + HEAD_DIM) & (row < inside + 2 * HEAD_DIM), queries, none)
        keys = k_ref[rows_of(g), 128 * p : 128 * p + 256]
        return jnp.dot(keys, jnp.concatenate([first, second], axis=1), preferred_element_type=F32)

    def weigh(g, scores):
        every = 8 if g < 3 else 4
        shape = scores.shape
        key_token = lax.broadcasted_iota(jnp.int32, shape, 0) % every
        same = key_token == lax.broadcasted_iota(jnp.int32, shape, 1) % every
        scores = jnp.where(same, scores, -1e30)
        top = jnp.max(scores, axis=0, keepdims=True)
        return jnp.exp2(scores - top).astype(BF16)

    def value(g, p, weights):
        at = 2 * HEAD_DIM * p
        tail = jnp.where(lax.broadcasted_iota(jnp.int32, (AUG - HEAD_DIM, weights.shape[0]), 0) == 0, 1.0, 0.0)
        first = vt_ref[at : at + HEAD_DIM, rows_of(g)]
        second = vt_ref[at + HEAD_DIM : at + 2 * HEAD_DIM, rows_of(g)]
        values = jnp.concatenate([first, tail, second, tail], axis=0).astype(BF16)
        return jnp.dot(values, weights, preferred_element_type=F32)

    def finish(g, p, total):
        at = 2 * HEAD_DIM * p
        first = total[:HEAD_DIM, :128] / total[HEAD_DIM : HEAD_DIM + 1, :128]
        second = total[AUG : AUG + HEAD_DIM, 128:] / total[AUG + HEAD_DIM : AUG + HEAD_DIM + 1, 128:]
        both = jnp.concatenate([first, second], axis=0).astype(BF16)
        att_ref[at : at + 2 * HEAD_DIM, g * 128 : g * 128 + 128] = both

    order = [(g, p) for g in range(4) for p in range(8)]
    apart = 4
    scores, totals = {}, {}
    for i in range(len(order) + 2 * apart):
        if i < len(order):
            scores[i] = score(*order[i])
        j = i - apart
        if 0 <= j < len(order):
            g, p = order[j]
            totals[j] = value(g, p, weigh(g, scores.pop(j)))
        k = i - 2 * apart
        if 0 <= k < len(order):
            finish(*order[k], totals.pop(k))

    projected = lax.dot_general(att_ref[:, :ROWS], wo_ref[...], TN, preferred_element_type=F32)
    x_ref[...] = x_ref[...] + mod_ref[5:6, :] * projected
    for f in range(16):
        for i in range(7):
            at = ((i // 2 * 16) + f) * 8 + i % 2 * 4 if i < 6 else 384 + 4 * f
            out_ref[f, i] = x_ref[at : at + 4, :].astype(BF16)


def temporal(mid, mod, w, wo):
    return pl.pallas_call(
        temporal_kernel,
        in_specs=[VMEM] * 4,
        out_specs=VMEM,
        out_shape=jax.ShapeDtypeStruct((16, 7, 4, WIDTH), BF16),
        scratch_shapes=[
            pltpu.VMEM((ROWS, WIDTH), F32),
            pltpu.VMEM((WIDTH, PADDED), BF16),
            pltpu.VMEM((ROWS, WIDTH), BF16),
            pltpu.VMEM((WIDTH, ROWS), F32),
            pltpu.VMEM((WIDTH, PADDED), BF16),
        ],
        compiler_params=params(24),
        cost_estimate=pl.CostEstimate(flops=6_000_000_000, bytes_accessed=14_000_000, transcendentals=1_000_000),
        name="temporal_block",
    )(mid, mod, w, wo)


def local(clip, modulation, w_qkv_s, w_out_s, w_qkv_t, w_out_t):
    own = clip[0]
    core = (lax.axis_index("head") % 2).astype(jnp.int32).reshape(1)
    swap_chip = [(0, 2), (1, 3), (2, 0), (3, 1)]
    swap_core = [(0, 1), (1, 0), (2, 3), (3, 2)]
    peer = lax.ppermute(own, "head", swap_core)
    there = lax.ppermute(own, "head", swap_chip)
    q, acc, top, mod, w = near(core, own, peer, modulation, w_qkv_s)
    there, q = lax.optimization_barrier((there, q))
    k1, vt1 = project(there, mod, w)
    there_peer = lax.ppermute(there, "head", swap_core)
    mine, theirs, w_t = far(core, there_peer, mod, w, k1, vt1, q, acc, top, w_qkv_t)
    other = lax.ppermute(theirs, "head", swap_core)
    middle = join(core, mine, other, own, mod, w_out_s)
    block = lax.all_to_all(middle, "tm", split_axis=0, concat_axis=0, tiled=True)
    done = temporal(block, modulation, w_t, w_out_t)
    back = lax.all_to_all(done, "tm", split_axis=0, concat_axis=0, tiled=True)
    return back.reshape(1, ROWS, WIDTH)


def solution(mesh):
    placed = (P(("dp", "tm"), "head", None), P("dp", None), P(), P(), P(), P())
    return jax.shard_map(
        local, mesh=mesh, in_specs=placed, out_specs=P(("dp", "tm"), "head", None), check_vma=False
    )
```

time: 107 us -> 98.5 us (0.921)
  local copies, waits for them, and re-layouts: 7.98 us -> 3.23 us
  blocking collectives: 48.3 us -> 44.8 us
  waiting for transfers between devices: 3.97 us -> 6.3 us
  Pallas kernels: 42.1 us -> 40.4 us
    unnamed x22 -> x12, local copies, waits for them, and re-layouts: 6.92 us -> 2.03 us
    pallas_call x3, Pallas kernels: 32 us -> 29.9 us  [the longest x1 17.4 us: near(): pl.pallas_call(near_kernel, in_specs=[SMEM, HBM, VMEM, HBM, HBM], out_spe...]
    ppermute x1, waiting for transfers between devices: 2.33 us -> 4.36 us  [local(): there = lax.ppermute(own, 'head', swap_chip)]
    all_to_all x1, blocking collectives: 21.2 us -> 19.4 us  [local(): back = lax.all_to_all(done, 'tm', split_axis=0, concat_axis=0, tiled=True)]
    all_to_all x1, blocking collectives: 27.1 us -> 25.4 us  [local(): lax.all_to_all(middle, 'tm', split_axis=0, concat_axis=0, tiled=True)]
  transfers between devices with their start and end apart: 4 -> 4, of which waited for: 2 -> 3; matrix products, arithmetic and copies ran while one was open for 0% -> 0% of each run, Pallas kernels for 18% -> 20%
where the time goes in v4:
time: 98.5 us; the launch traced here: 98.2 us
  blocking collectives  44.8 us (45%)
  Pallas kernels  40.4 us (41%)
  waiting for transfers between devices  6.3 us (6%)
  starting transfers between devices  3.49 us (4%)
  local copies, waits for them, and re-layouts  3.23 us (3%)
    all_to_all x1, blocking collectives, local(): lax.all_to_all(middle, 'tm', split_axis=0, concat_axis=0, tiled=True)  25.4 us
    all_to_all x1, blocking collectives, local(): back = lax.all_to_all(done, 'tm', split_axis=0, concat_axis=0, tiled=True)  19.4 us
    pallas_call x1, Pallas kernels, near(): pl.pallas_call(near_kernel, in_specs=[SMEM, HBM, VMEM, HBM, HBM], out_spe...  17.4 us
    pallas_call x1, Pallas kernels, far(): pl.pallas_call(far_kernel, in_specs=[SMEM] + [VMEM] * 8 + [HBM], out_spec...  10.1 us
    pallas_call x1, Pallas kernels, temporal(): pl.pallas_call(temporal_kernel, in_specs=[VMEM] * 4, out_specs=VMEM, out_...  8.66 us
    ppermute x1, waiting for transfers between devices, local(): there = lax.ppermute(own, 'head', swap_chip)  4.36 us
    ppermute x1, starting transfers between devices, local(): there = lax.ppermute(own, 'head', swap_chip)  3.11 us
    pallas_call x1, Pallas kernels, project(): pl.pallas_call(project_kernel, in_specs=[VMEM] * 3, out_specs=[VMEM] * 2,...  2.4 us
  transfers between devices with their start and end apart: 4, of which 3 were waited for; matrix products, arithmetic and copies ran while one was open for 0% of the time, Pallas kernels for 20%

profile of v4, /device:TPU:0, one launch (start us, length us, event | category | flops | bytes accessed | tf_op | source)
XLA Modules:
  0.0 98.2 jit_solution(10569590009947241822)
XLA Ops:
  0.0 0.0 collective-permute-start.1
  0.0 3.1 %collective-permute-start = (bf16[448,1152]{1,0:T(8,128)(2,1)}, bf16[448,1152]{1,0:T(8,128)(2,1)S(1)}, u32[]{:S(2)}, u32[]{:S(2)}) collective-permute-start(bf16[448,1152]{1,0:T(8,128)(2,1)} %bitcast.3), channel_id=1, source_target_pairs={{0,2},{1,3},{2,0},{3,1},{4,6},{5,7},{6,4},{7,5},{8,10},{9,11},{10,... | collective-permute-start | bytes 3096584 | tf_op jit(solution)/shard_map/ppermute | solution.py:378
  3.1 0.0 collective-permute-done.1.xp_ref
  3.1 0.0 copy-start
  3.1 1.2 %copy-done = bf16[1,448,1152]{2,1,0:T(8,128)(2,1)S(1)} copy-done((bf16[1,448,1152]{2,1,0:T(8,128)(2,1)S(1)}, bf16[1,448,1152]{2,1,0:T(8,128)(2,1)}, u32[]{:S(2)}) %copy-start) | copy-done | bytes 1032216
  4.4 0.0 copy-start.3
  4.4 0.8 copy-done.3
  5.1 17.4 %near_tokens.1 = (bf16[896,640]{1,0:T(8,128)(2,1)S(1)}, f32[8,80,896]{2,1,0:T(8,128)S(1)}, f32[8,8,896]{2,1,0:T(8,128)S(1)}, f32[6,1152]{1,0:T(8,128)S(1)}, bf16[1152,1280]{1,0:T(8,128)(2,1)S(1)}) custom-call(s32[1]{0:T(128)} %bitcast.core_ref, bf16[448,1152]{1,0:T(8,128)(2,1)S(1)} %bitcast.4, bf16[448,1152]{1,0:T(8,128)(2,1)S(1)} %collective-permute-done.1.xp_ref, ...), custom_call_target="tpu_custom_call" | custom-call | flops 1000000 | bytes 100000 | tf_op jit(solution)/shard_map/near_tokens/pallas_call | solution.py:151
  22.6 4.4 %collective-permute-done.x_ref = bf16[448,1152]{1,0:T(8,128)(2,1)S(1)} collective-permute-done((bf16[448,1152]{1,0:T(8,128)(2,1)}, bf16[448,1152]{1,0:T(8,128)(2,1)S(1)}, u32[]{:S(2)}, u32[]{:S(2)}) %collective-permute-start) | collective-permute-done | bytes 1032224 | tf_op jit(solution)/shard_map/ppermute | solution.py:378
  26.9 0.0 collective-permute-start.2
  26.9 2.4 %far_keys.1 = (bf16[448,640]{1,0:T(8,128)(2,1)S(1)}, f32[640,448]{1,0:T(8,128)S(1)}) custom-call(bf16[448,1152]{1,0:T(8,128)(2,1)S(1)} %collective-permute-done.x_ref, f32[6,1152]{1,0:T(8,128)S(1)} %get-tuple-element.19.mod_ref, bf16[1152,1280]{1,0:T(8,128)(2,1)S(1)} %get-tuple-element.20.w_ref), custom_call_target="tpu_custom_call" | custom-call | flops 1000000 | bytes 100000 | tf_op jit(solution)/shard_map/far_keys/pallas_call | solution.py:182
  29.4 0.2 collective-permute-done.2.x_ref
  29.6 0.0 copy-start.1
  29.6 0.0 copy-start.2
  29.6 10.1 %far_tokens.1 = (bf16[576,448]{1,0:T(8,128)(2,1)S(1)}, bf16[576,512]{1,0:T(8,128)(2,1)S(1)}, bf16[1152,3456]{1,0:T(8,128)(2,1)S(1)}) custom-call(s32[1]{0:T(128)} %bitcast.core_ref, bf16[448,1152]{1,0:T(8,128)(2,1)S(1)} %collective-permute-done.2.x_ref, f32[6,1152]{1,0:T(8,128)S(1)} %get-tuple-element.19.mod_ref, ...), custom_call_target="tpu_custom_call" | custom-call | flops 17999998976 | bytes 10000000 | tf_op jit(solution)/shard_map/far_tokens/pallas_call | solution.py:236
  39.6 0.4 collective-permute-start.3
  40.0 1.7 %collective-permute-done.3.other_ref = bf16[576,512]{1,0:T(8,128)(2,1)S(1)} collective-permute-done((bf16[576,512]{1,0:T(8,128)(2,1)S(1)}, bf16[576,512]{1,0:T(8,128)(2,1)S(1)}, u32[]{:S(2)}, u32[]{:S(2)}) %collective-permute-start.3) | collective-permute-done | bytes 589856 | tf_op jit(solution)/shard_map/ppermute | solution.py:384
  41.7 0.0 copy-done.1
  41.7 0.0 copy-done.2
  41.7 0.0 copy-start.4
  41.7 0.0 copy-start.5
  41.7 1.8 %spatial_out.1 = bf16[16,7,4,1152]{3,2,1,0:T(4,128)(2,1)S(1)} custom-call(s32[1]{0:T(128)} %bitcast.core_ref, bf16[576,448]{1,0:T(8,128)(2,1)S(1)} %get-tuple-element.26.mine_ref, bf16[576,512]{1,0:T(8,128)(2,1)S(1)} %collective-permute-done.3.other_ref, bf16[448,1152]{1,0:T(8,128)(2,1)S(1)} %bitcast.5, f32[6,1152]{1,0:T(8,128)S(1)} %get-tuple-element.19.mod_ref, ...), custom_call_target="tpu_custom_call" | custom-call | flops 1200000000 | bytes 6000000 | tf_op jit(solution)/shard_map/spatial_out/pallas_call | solution.py:269
  43.6 25.4 %all_to_all.10.mid_ref = bf16[16,7,4,1152]{3,2,1,0:T(4,128)(2,1)S(1)} all-to-all(bf16[16,7,4,1152]{3,2,1,0:T(4,128)(2,1)S(1)} %spatial_out.1), channel_id=1, replica_groups=mesh['dp'=2,'tm'=16,'head'=4] {'tm'}, dimensions={0} | all-to-all | bytes 2064384 | tf_op jit(solution)/shard_map/all_to_all | solution.py:386
  68.9 0.0 copy-done.4
  68.9 0.0 copy-done.5
  68.9 8.7 %temporal_block.1 = bf16[16,7,4,1152]{3,2,1,0:T(4,128)(2,1)S(1)} custom-call(bf16[16,7,4,1152]{3,2,1,0:T(4,128)(2,1)S(1)} %all_to_all.10.mid_ref, f32[6,1152]{1,0:T(8,128)S(1)} %copy-done.4, bf16[1152,3456]{1,0:T(8,128)(2,1)S(1)} %get-tuple-element.28.w_ref, bf16[1152,1152]{1,0:T(8,128)(2,1)S(1)} %copy-done.5), custom_call_target="tpu_custom_call" | custom-call | flops 6000000000 | bytes 14000000 | tf_op jit(solution)/shard_map/temporal_block/pallas_call | solution.py:354
  77.6 19.4 %all_to_all.11 = bf16[16,7,4,1152]{3,2,1,0:T(4,128)(2,1)S(1)} all-to-all(bf16[16,7,4,1152]{3,2,1,0:T(4,128)(2,1)S(1)} %temporal_block.1), channel_id=1, replica_groups=mesh['dp'=2,'tm'=16,'head'=4] {'tm'}, dimensions={0} | all-to-all | bytes 2064384 | tf_op jit(solution)/shard_map/all_to_all | solution.py:388
  97.0 1.2 %reshape.7 = bf16[1,448,1152]{2,1,0:T(8,128)(2,1)} reshape(bf16[16,7,4,1152]{3,2,1,0:T(4,128)(2,1)S(1)} %all_to_all.11) | data formatting | bytes 2064384 | tf_op jit(solution)/shard_map/reshape | solution.py:389
Async XLA Ops:
  0.0 3.1 %collective-permute-start.1 = (bf16[448,1152]{1,0:T(8,128)(2,1)}, bf16[448,1152]{1,0:T(8,128)(2,1)S(1)}, u32[]{:S(2)}, u32[]{:S(2)}) collective-permute-start(bf16[448,1152]{1,0:T(8,128)(2,1)} %bitcast.2), channel_id=1, source_target_pairs={{0,1},{1,0},{2,3},{3,2},{4,5},{5,4},{6,7},{7,6},{8,9},{9,8},{10,11... | collective-permute-start | bytes 3096584 | tf_op jit(solution)/shard_map/ppermute | solution.py:377
  0.0 26.9 %collective-permute-start = (bf16[448,1152]{1,0:T(8,128)(2,1)}, bf16[448,1152]{1,0:T(8,128)(2,1)S(1)}, u32[]{:S(2)}, u32[]{:S(2)}) collective-permute-start(bf16[448,1152]{1,0:T(8,128)(2,1)} %bitcast.3), channel_id=1, source_target_pairs={{0,2},{1,3},{2,0},{3,1},{4,6},{5,7},{6,4},{7,5},{8,10},{9,11},{10,... | collective-permute-start | bytes 3096584 | tf_op jit(solution)/shard_map/ppermute | solution.py:378
  3.1 1.2 %copy-start = (bf16[1,448,1152]{2,1,0:T(8,128)(2,1)S(1)}, bf16[1,448,1152]{2,1,0:T(8,128)(2,1)}, u32[]{:S(2)}) copy-start(bf16[1,448,1152]{2,1,0:T(8,128)(2,1)} %param.6) | copy-start | bytes 3096580
  4.4 0.8 copy-start.3
  26.9 2.6 %collective-permute-start.2 = (bf16[448,1152]{1,0:T(8,128)(2,1)S(1)}, bf16[448,1152]{1,0:T(8,128)(2,1)S(1)}, u32[]{:S(2)}, u32[]{:S(2)}) collective-permute-start(bf16[448,1152]{1,0:T(8,128)(2,1)S(1)} %collective-permute-done.x_ref), channel_id=1, source_target_pairs={{0,1},{1,0},{2,3},{3,2},{4,5},{5,4},{6,7},{7,6},{8,9},{9,8},{10,11... | collective-permute-start | bytes 3096584 | tf_op jit(solution)/shard_map/ppermute | solution.py:382
  29.6 12.2 %copy-start.1 = (bf16[1,448,1152]{2,1,0:T(8,128)(2,1)S(1)}, bf16[1,448,1152]{2,1,0:T(8,128)(2,1)}, u32[]{:S(2)}) copy-start(bf16[1,448,1152]{2,1,0:T(8,128)(2,1)} %param.6) | copy-start | bytes 3096580
  29.6 12.2 %copy-start.2 = (bf16[1152,1152]{1,0:T(8,128)(2,1)S(1)}, bf16[1152,1152]{1,0:T(8,128)(2,1)}, u32[]{:S(2)}) copy-start(bf16[1152,1152]{1,0:T(8,128)(2,1)} %wo_ref.2) | copy-start | bytes 7962628
  39.6 2.1 %collective-permute-start.3 = (bf16[576,512]{1,0:T(8,128)(2,1)S(1)}, bf16[576,512]{1,0:T(8,128)(2,1)S(1)}, u32[]{:S(2)}, u32[]{:S(2)}) collective-permute-start(bf16[576,512]{1,0:T(8,128)(2,1)S(1)} %get-tuple-element.27), channel_id=1, source_target_pairs={{0,1},{1,0},{2,3},{3,2},{4,5},{5,4},{6,7},{7,6},{8,9},{9,8},{10,11... | collective-permute-start | bytes 1769480 | tf_op jit(solution)/shard_map/ppermute | solution.py:384
  41.7 27.2 %copy-start.4 = (f32[6,1152]{1,0:T(8,128)S(1)}, f32[6,1152]{1,0:T(8,128)}, u32[]{:S(2)}) copy-start(f32[6,1152]{1,0:T(8,128)} %mod_ref.1) | copy-start | bytes 82948
  41.7 27.2 %copy-start.5 = (bf16[1152,1152]{1,0:T(8,128)(2,1)S(1)}, bf16[1152,1152]{1,0:T(8,128)(2,1)}, u32[]{:S(2)}) copy-start(bf16[1152,1152]{1,0:T(8,128)(2,1)} %wo_ref.3) | copy-start | bytes 7962628
